TPU v7x, 32 devices: a whole 2x2x4 slice. The times are simulated.
32 devices in a mesh: blk: 16 (over z, y, core), rhs: 2 (over x).
Axes of the slice: x: 2, y: 2, z: 4, core: 2. Of those that a mesh axis runs over, the one named last changes fastest.
Arguments:
- directions: bfloat16 [32768, 256], P('blk', 'rhs'), may hold values from -6 to 6
- axial_pos: bfloat16 [32768], P('blk'), may hold values from 0 to 8
- azimuth: bfloat16 [32768], P('blk'), may hold values from -3.140625 to 3.140625
- panel_area: bfloat16 [32768], P('blk'), may hold values from 0.5 to 2
Outputs:
- product: float32 [32768, 256], P('blk', 'rhs')
- gram: float32 [256, 256], P(None, 'rhs')
All inputs are finite; a program needn't handle non-finite values.
Results may differ from a plain program's by a relative error of at most 0.0029.
Values may be sent and summed in bfloat16 or wider, within the bound.
A program may use at most 64 MiB of HBM per device.

v0:
```python
import math

import jax
import jax.numpy as jnp
from jax import lax
from jax.sharding import PartitionSpec as P

ROUNDS = 3


def shifted(value, axis, steps):
    count = lax.axis_size(axis)
    pairs = [(source, (source + steps) % count) for source in range(count)]
    return lax.ppermute(value, axis, pairs)


def kernel_tile(row_geom, col_geom, count):
    row_axial, row_cos, row_sin, row_weight = row_geom
    col_axial, col_cos, col_sin, col_weight = col_geom
    delta_a = row_axial[:, None] - col_axial[None, :]
    delta_c = row_cos[:, None] - col_cos[None, :]
    delta_s = row_sin[:, None] - col_sin[None, :]
    square = delta_a * delta_a + delta_c * delta_c + delta_s * delta_s
    weights = row_weight[:, None] * col_weight[None, :]
    value = weights * lax.rsqrt(square + 0.01) / jnp.sqrt(jnp.float32(count))
    return value.astype(jnp.bfloat16)


def panel_points(axial_pos, azimuth, panel_area):
    angle_f = azimuth.astype(jnp.float32)
    return (
        axial_pos.astype(jnp.float32),
        jnp.cos(angle_f),
        jnp.sin(angle_f),
        panel_area.astype(jnp.float32),
    )


def apply_tile(home_geom, other_geom, other_dirs, home_dirs, with_back, count):
    row_total = home_dirs.shape[0]
    width = home_dirs.shape[1]
    row_step = math.gcd(row_total, 512)
    blocks = row_total // row_step
    split_geom = tuple((part.reshape(blocks, row_step) for part in home_geom))
    split_dirs = home_dirs.reshape(blocks, row_step, width)

    def step_fn(carried, item):
        row_axial, row_cos, row_sin, row_weight, row_dirs = item
        values = kernel_tile((row_axial, row_cos, row_sin, row_weight), other_geom, count)
        forward = jnp.dot(values, other_dirs, preferred_element_type=jnp.float32)
        if with_back:
            carried = carried + lax.dot_general(
                values, row_dirs, (((0,), (0,)), ((), ())), preferred_element_type=jnp.float32
            )
        return (carried, forward)

    start = jnp.zeros((other_dirs.shape[0], width), jnp.float32)
    backward, pieces = lax.scan(step_fn, start, split_geom + (split_dirs,))
    return (pieces.reshape(row_total, other_dirs.shape[1]), backward)


def shards(directions, axial_pos, azimuth, panel_area):
    count = axial_pos.shape[0]
    home_geom = panel_points(axial_pos, azimuth, panel_area)
    whole = lax.all_gather(directions, "rhs", axis=1, tiled=True)
    product, unused_back = apply_tile(home_geom, home_geom, directions, directions, False, count)
    for shift_by in range(1, ROUNDS + 1):
        guest_dirs, guest_axial, guest_angle, guest_area = shifted(
            (directions, axial_pos, azimuth, panel_area), "blk", shift_by
        )
        forward, backward = apply_tile(
            home_geom,
            panel_points(guest_axial, guest_angle, guest_area),
            guest_dirs,
            directions,
            True,
            count,
        )
        product = product + forward
        product = product + shifted(backward, "blk", -shift_by)
    partial_value = jnp.dot(whole.astype(jnp.float32).T, product, precision=lax.Precision.HIGHEST)
    gram = lax.psum(partial_value, "blk") / (count * lax.axis_size("blk"))
    return (product, gram)


def solution(mesh):
    in_specs = (P("blk", "rhs"), P("blk"), P("blk"), P("blk"))
    out_specs = (P("blk", "rhs"), P(None, "rhs"))
    return jax.shard_map(shards, mesh=mesh, in_specs=in_specs, out_specs=out_specs, check_vma=False)
```

profile of v0, /device:TPU:0, one launch (start us, length us, event | category | flops | bytes accessed | tf_op | source)
XLA Modules:
  0.0 249.3 jit_solution(666603940600611141)
XLA Ops:
  7.2 0.5 collective-permute-start.2
  7.7 2.6 %collective-permute-start.7 = (bf16[2048]{0:T(1024)(128)(2,1)}, bf16[2048]{0:T(1024)(128)(2,1)S(1)}, u32[]{:S(2)}, u32[]{:S(2)}) collective-permute-start(bf16[2048]{0:T(1024)(128)(2,1)} %param.14), channel_id=1, source_target_pairs={{0,4},{2,6},{4,8},{6,10},{8,12},{10,14},{12,16},{14,18},{16,20},{1... | collective-permute-start | bytes 12296 | tf_op jit(solution)/shard_map/ppermute | solution.py:14
  10.3 1.3 collective-permute-start.3
  11.7 0.4 collective-permute-start
  12.1 1.3 collective-permute-start.1
  13.3 0.7 convert_sine_fusion.3
  14.1 0.7 reshape.90
  14.8 0.7 reshape.91
  15.5 0.7 convert_element_type.49
  16.2 0.7 convert_element_type.50
  16.9 1.6 collective-permute-start.5
  18.5 3.3 %collective-permute-done = bf16[2048]{0:T(1024)(128)(2,1)S(1)} collective-permute-done((bf16[2048]{0:T(1024)(128)(2,1)}, bf16[2048]{0:T(1024)(128)(2,1)S(1)}, u32[]{:S(2)}, u32[]{:S(2)}) %collective-permute-start) | collective-permute-done | bytes 4128 | tf_op jit(solution)/shard_map/ppermute | solution.py:14
  21.9 2.5 %collective-permute-start.10 = (bf16[2048]{0:T(1024)(128)(2,1)}, bf16[2048]{0:T(1024)(128)(2,1)S(1)}, u32[]{:S(2)}, u32[]{:S(2)}) collective-permute-start(bf16[2048]{0:T(1024)(128)(2,1)} %param.15), channel_id=1, source_target_pairs={{0,6},{2,8},{4,10},{6,12},{8,14},{10,16},{12,18},{14,20},{16,22},{... | collective-permute-start | bytes 12296 | tf_op jit(solution)/shard_map/ppermute | solution.py:14
  24.5 3.8 %collective-permute-done.6 = bf16[2048]{0:T(1024)(128)(2,1)S(1)} collective-permute-done((bf16[2048]{0:T(1024)(128)(2,1)}, bf16[2048]{0:T(1024)(128)(2,1)S(1)}, u32[]{:S(2)}, u32[]{:S(2)}) %collective-permute-start.6) | collective-permute-done | bytes 4128 | tf_op jit(solution)/shard_map/ppermute | solution.py:14
  28.4 0.7 collective-permute-start.13
  29.1 0.4 collective-permute-done.11
  29.5 0.1 broadcast.51.clone.2
  29.6 25.9 %while.50 = (s32[]{:T(128)}, f32[2048,128]{1,0:T(8,128)}, f32[4,512,128]{2,1,0:T(8,128)S(1)}, f32[4,512]{1,0:T(4,128)S(1)}, f32[2048]{0:T(1024)S(1)}, /*index=5*...) while((s32[]{:T(128)}, f32[2048,128]{1,0:T(8,128)}, ...), condition=%wide.region_3.4_spmd.clone, body=%wide.region_2.3_spmd.clone.sunk | while | flops 564658176 | bytes 3113635 | solution.py:58
  29.6 2.0 fusion.52
  31.7 4.1 %convolution_add_fusion.6 = f32[2048,128]{1,0:T(8,128)} fusion(f32[2048,128]{1,0:T(8,128)} %get-tuple-element.964, f32[2048]{0:T(1024)S(1)} %get-tuple-element.988, f32[512]{0:T(512)S(1)} %bitcast.121, f32[2048]{0:T(1024)S(1)} %get-tuple-element.986, f32[512]{0:T(512)S(1)} %bitcast.123, f32[2048]{0:T(1024)S(1)} %get-tuple-element.984, ...), kind=kOutput, calls=%fused_computation.11.clone.1 | convolution fusion | flops 282591232 | bytes 2269697 | tf_op jit(solution)/shard_map/while/body/eval_jaxpr/dot_general | solution.py:52
  35.8 2.0 fusion.52
  37.8 4.5 %convolution_add_fusion.6 = f32[2048,128]{1,0:T(8,128)} fusion(f32[2048,128]{1,0:T(8,128)} %get-tuple-element.964, f32[2048]{0:T(1024)S(1)} %get-tuple-element.988, f32[512]{0:T(512)S(1)} %bitcast.121, f32[2048]{0:T(1024)S(1)} %get-tuple-element.986, f32[512]{0:T(512)S(1)} %bitcast.123, f32[2048]{0:T(1024)S(1)} %get-tuple-element.984, ...), kind=kOutput, calls=%fused_computation.11.clone.1 | convolution fusion | flops 282591232 | bytes 2269697 | tf_op jit(solution)/shard_map/while/body/eval_jaxpr/dot_general | solution.py:52
  42.4 2.0 fusion.52
  44.4 4.5 %convolution_add_fusion.6 = f32[2048,128]{1,0:T(8,128)} fusion(f32[2048,128]{1,0:T(8,128)} %get-tuple-element.964, f32[2048]{0:T(1024)S(1)} %get-tuple-element.988, f32[512]{0:T(512)S(1)} %bitcast.121, f32[2048]{0:T(1024)S(1)} %get-tuple-element.986, f32[512]{0:T(512)S(1)} %bitcast.123, f32[2048]{0:T(1024)S(1)} %get-tuple-element.984, ...), kind=kOutput, calls=%fused_computation.11.clone.1 | convolution fusion | flops 282591232 | bytes 2269697 | tf_op jit(solution)/shard_map/while/body/eval_jaxpr/dot_general | solution.py:52
  48.9 2.0 fusion.52
  51.0 4.5 %convolution_add_fusion.6 = f32[2048,128]{1,0:T(8,128)} fusion(f32[2048,128]{1,0:T(8,128)} %get-tuple-element.964, f32[2048]{0:T(1024)S(1)} %get-tuple-element.988, f32[512]{0:T(512)S(1)} %bitcast.121, f32[2048]{0:T(1024)S(1)} %get-tuple-element.986, f32[512]{0:T(512)S(1)} %bitcast.123, f32[2048]{0:T(1024)S(1)} %get-tuple-element.984, ...), kind=kOutput, calls=%fused_computation.11.clone.1 | convolution fusion | flops 282591232 | bytes 2269697 | tf_op jit(solution)/shard_map/while/body/eval_jaxpr/dot_general | solution.py:52
  55.5 1.8 collective-permute-start.4
  57.2 0.8 copy-done.2
  58.0 0.1 broadcast.51.clone.1
  58.1 30.0 %while.51 = (s32[]{:T(128)}, f32[2048,128]{1,0:T(8,128)}, f32[4,512,128]{2,1,0:T(8,128)S(1)}, f32[4,512]{1,0:T(4,128)S(1)}, f32[2048]{0:T(1024)S(1)}, /*index=5*...) while((s32[]{:T(128)}, f32[2048,128]{1,0:T(8,128)}, ...), condition=%wide.region_5.6_spmd.clone, body=%wide.region_4.5_spmd.clone.sunk | while | flops 564658176 | bytes 3113635 | solution.py:58
  58.2 3.1 %fusion.55 = f32[4,512,128]{2,1,0:T(8,128)S(1)} fusion(f32[4,512,128]{2,1,0:T(8,128)S(1)} %get-tuple-element.920, s32[]{:T(128)} %get-tuple-element.918, bf16[2048,128]{1,0:T(8,128)(2,1)} %get-tuple-element.945, f32[2048]{0:T(1024)S(1)} %get-tuple-element.943, f32[512]{0:T(512)S(1)} %bitcast.124, f32[2048]{0:T(1024)S(1)} %get-tuple-element.941, ...), kind=kOutput, calls=%fused_computation.28.clone.1 | convolution fusion | flops 282066944 | bytes 827396 | tf_op jit(solution)/shard_map/while/body/eval_jaxpr/dot_general | solution.py:50
  61.2 4.1 %convolution_add_fusion.7 = f32[2048,128]{1,0:T(8,128)} fusion(f32[2048,128]{1,0:T(8,128)} %get-tuple-element.919, f32[2048]{0:T(1024)S(1)} %get-tuple-element.943, f32[512]{0:T(512)S(1)} %bitcast.125, f32[2048]{0:T(1024)S(1)} %get-tuple-element.941, f32[512]{0:T(512)S(1)} %bitcast.127, f32[2048]{0:T(1024)S(1)} %get-tuple-element.939, ...), kind=kOutput, calls=%fused_computation.26.clone.1 | convolution fusion | flops 282591232 | bytes 2269697 | tf_op jit(solution)/shard_map/while/body/eval_jaxpr/dot_general | solution.py:52
  65.4 3.1 %fusion.55 = f32[4,512,128]{2,1,0:T(8,128)S(1)} fusion(f32[4,512,128]{2,1,0:T(8,128)S(1)} %get-tuple-element.920, s32[]{:T(128)} %get-tuple-element.918, bf16[2048,128]{1,0:T(8,128)(2,1)} %get-tuple-element.945, f32[2048]{0:T(1024)S(1)} %get-tuple-element.943, f32[512]{0:T(512)S(1)} %bitcast.124, f32[2048]{0:T(1024)S(1)} %get-tuple-element.941, ...), kind=kOutput, calls=%fused_computation.28.clone.1 | convolution fusion | flops 282066944 | bytes 827396 | tf_op jit(solution)/shard_map/while/body/eval_jaxpr/dot_general | solution.py:50
  68.4 4.5 %convolution_add_fusion.7 = f32[2048,128]{1,0:T(8,128)} fusion(f32[2048,128]{1,0:T(8,128)} %get-tuple-element.919, f32[2048]{0:T(1024)S(1)} %get-tuple-element.943, f32[512]{0:T(512)S(1)} %bitcast.125, f32[2048]{0:T(1024)S(1)} %get-tuple-element.941, f32[512]{0:T(512)S(1)} %bitcast.127, f32[2048]{0:T(1024)S(1)} %get-tuple-element.939, ...), kind=kOutput, calls=%fused_computation.26.clone.1 | convolution fusion | flops 282591232 | bytes 2269697 | tf_op jit(solution)/shard_map/while/body/eval_jaxpr/dot_general | solution.py:52
  73.0 3.1 %fusion.55 = f32[4,512,128]{2,1,0:T(8,128)S(1)} fusion(f32[4,512,128]{2,1,0:T(8,128)S(1)} %get-tuple-element.920, s32[]{:T(128)} %get-tuple-element.918, bf16[2048,128]{1,0:T(8,128)(2,1)} %get-tuple-element.945, f32[2048]{0:T(1024)S(1)} %get-tuple-element.943, f32[512]{0:T(512)S(1)} %bitcast.124, f32[2048]{0:T(1024)S(1)} %get-tuple-element.941, ...), kind=kOutput, calls=%fused_computation.28.clone.1 | convolution fusion | flops 282066944 | bytes 827396 | tf_op jit(solution)/shard_map/while/body/eval_jaxpr/dot_general | solution.py:50
  76.0 4.5 %convolution_add_fusion.7 = f32[2048,128]{1,0:T(8,128)} fusion(f32[2048,128]{1,0:T(8,128)} %get-tuple-element.919, f32[2048]{0:T(1024)S(1)} %get-tuple-element.943, f32[512]{0:T(512)S(1)} %bitcast.125, f32[2048]{0:T(1024)S(1)} %get-tuple-element.941, f32[512]{0:T(512)S(1)} %bitcast.127, f32[2048]{0:T(1024)S(1)} %get-tuple-element.939, ...), kind=kOutput, calls=%fused_computation.26.clone.1 | convolution fusion | flops 282591232 | bytes 2269697 | tf_op jit(solution)/shard_map/while/body/eval_jaxpr/dot_general | solution.py:52
  80.6 3.1 %fusion.55 = f32[4,512,128]{2,1,0:T(8,128)S(1)} fusion(f32[4,512,128]{2,1,0:T(8,128)S(1)} %get-tuple-element.920, s32[]{:T(128)} %get-tuple-element.918, bf16[2048,128]{1,0:T(8,128)(2,1)} %get-tuple-element.945, f32[2048]{0:T(1024)S(1)} %get-tuple-element.943, f32[512]{0:T(512)S(1)} %bitcast.124, f32[2048]{0:T(1024)S(1)} %get-tuple-element.941, ...), kind=kOutput, calls=%fused_computation.28.clone.1 | convolution fusion | flops 282066944 | bytes 827396 | tf_op jit(solution)/shard_map/while/body/eval_jaxpr/dot_general | solution.py:50
  83.6 4.5 %convolution_add_fusion.7 = f32[2048,128]{1,0:T(8,128)} fusion(f32[2048,128]{1,0:T(8,128)} %get-tuple-element.919, f32[2048]{0:T(1024)S(1)} %get-tuple-element.943, f32[512]{0:T(512)S(1)} %bitcast.125, f32[2048]{0:T(1024)S(1)} %get-tuple-element.941, f32[512]{0:T(512)S(1)} %bitcast.127, f32[2048]{0:T(1024)S(1)} %get-tuple-element.939, ...), kind=kOutput, calls=%fused_computation.26.clone.1 | convolution fusion | flops 282591232 | bytes 2269697 | tf_op jit(solution)/shard_map/while/body/eval_jaxpr/dot_general | solution.py:52
  88.1 2.3 collective-permute-start.9
  90.4 0.8 copy-done.1
  91.2 0.1 broadcast.51.clone
  91.3 30.0 %while.52 = (s32[]{:T(128)}, f32[2048,128]{1,0:T(8,128)}, f32[4,512,128]{2,1,0:T(8,128)S(1)}, f32[4,512]{1,0:T(4,128)S(1)}, f32[2048]{0:T(1024)S(1)}, /*index=5*...) while((s32[]{:T(128)}, f32[2048,128]{1,0:T(8,128)}, ...), condition=%wide.region_7.8_spmd.clone, body=%wide.region_6.7_spmd.clone.sunk | while | flops 564658176 | bytes 3113635 | solution.py:58
  91.3 3.1 %fusion.58 = f32[4,512,128]{2,1,0:T(8,128)S(1)} fusion(f32[4,512,128]{2,1,0:T(8,128)S(1)} %get-tuple-element.875, s32[]{:T(128)} %get-tuple-element.873, bf16[2048,128]{1,0:T(8,128)(2,1)} %get-tuple-element.900, f32[2048]{0:T(1024)S(1)} %get-tuple-element.898, f32[512]{0:T(512)S(1)} %bitcast.128, f32[2048]{0:T(1024)S(1)} %get-tuple-element.896, ...), kind=kOutput, calls=%fused_computation.43.clone.1 | convolution fusion | flops 282066944 | bytes 827396 | tf_op jit(solution)/shard_map/while/body/eval_jaxpr/dot_general | solution.py:50
  94.4 4.1 %convolution_add_fusion.8 = f32[2048,128]{1,0:T(8,128)} fusion(f32[2048,128]{1,0:T(8,128)} %get-tuple-element.874, f32[2048]{0:T(1024)S(1)} %get-tuple-element.898, f32[512]{0:T(512)S(1)} %bitcast.129, f32[2048]{0:T(1024)S(1)} %get-tuple-element.896, f32[512]{0:T(512)S(1)} %bitcast.131, f32[2048]{0:T(1024)S(1)} %get-tuple-element.894, ...), kind=kOutput, calls=%fused_computation.41.clone.1 | convolution fusion | flops 282591232 | bytes 2269697 | tf_op jit(solution)/shard_map/while/body/eval_jaxpr/dot_general | solution.py:52
  98.5 3.1 %fusion.58 = f32[4,512,128]{2,1,0:T(8,128)S(1)} fusion(f32[4,512,128]{2,1,0:T(8,128)S(1)} %get-tuple-element.875, s32[]{:T(128)} %get-tuple-element.873, bf16[2048,128]{1,0:T(8,128)(2,1)} %get-tuple-element.900, f32[2048]{0:T(1024)S(1)} %get-tuple-element.898, f32[512]{0:T(512)S(1)} %bitcast.128, f32[2048]{0:T(1024)S(1)} %get-tuple-element.896, ...), kind=kOutput, calls=%fused_computation.43.clone.1 | convolution fusion | flops 282066944 | bytes 827396 | tf_op jit(solution)/shard_map/while/body/eval_jaxpr/dot_general | solution.py:50
  101.6 4.5 %convolution_add_fusion.8 = f32[2048,128]{1,0:T(8,128)} fusion(f32[2048,128]{1,0:T(8,128)} %get-tuple-element.874, f32[2048]{0:T(1024)S(1)} %get-tuple-element.898, f32[512]{0:T(512)S(1)} %bitcast.129, f32[2048]{0:T(1024)S(1)} %get-tuple-element.896, f32[512]{0:T(512)S(1)} %bitcast.131, f32[2048]{0:T(1024)S(1)} %get-tuple-element.894, ...), kind=kOutput, calls=%fused_computation.41.clone.1 | convolution fusion | flops 282591232 | bytes 2269697 | tf_op jit(solution)/shard_map/while/body/eval_jaxpr/dot_general | solution.py:52
  106.1 3.1 %fusion.58 = f32[4,512,128]{2,1,0:T(8,128)S(1)} fusion(f32[4,512,128]{2,1,0:T(8,128)S(1)} %get-tuple-element.875, s32[]{:T(128)} %get-tuple-element.873, bf16[2048,128]{1,0:T(8,128)(2,1)} %get-tuple-element.900, f32[2048]{0:T(1024)S(1)} %get-tuple-element.898, f32[512]{0:T(512)S(1)} %bitcast.128, f32[2048]{0:T(1024)S(1)} %get-tuple-element.896, ...), kind=kOutput, calls=%fused_computation.43.clone.1 | convolution fusion | flops 282066944 | bytes 827396 | tf_op jit(solution)/shard_map/while/body/eval_jaxpr/dot_general | solution.py:50
  109.2 4.5 %convolution_add_fusion.8 = f32[2048,128]{1,0:T(8,128)} fusion(f32[2048,128]{1,0:T(8,128)} %get-tuple-element.874, f32[2048]{0:T(1024)S(1)} %get-tuple-element.898, f32[512]{0:T(512)S(1)} %bitcast.129, f32[2048]{0:T(1024)S(1)} %get-tuple-element.896, f32[512]{0:T(512)S(1)} %bitcast.131, f32[2048]{0:T(1024)S(1)} %get-tuple-element.894, ...), kind=kOutput, calls=%fused_computation.41.clone.1 | convolution fusion | flops 282591232 | bytes 2269697 | tf_op jit(solution)/shard_map/while/body/eval_jaxpr/dot_general | solution.py:52
  113.7 3.1 %fusion.58 = f32[4,512,128]{2,1,0:T(8,128)S(1)} fusion(f32[4,512,128]{2,1,0:T(8,128)S(1)} %get-tuple-element.875, s32[]{:T(128)} %get-tuple-element.873, bf16[2048,128]{1,0:T(8,128)(2,1)} %get-tuple-element.900, f32[2048]{0:T(1024)S(1)} %get-tuple-element.898, f32[512]{0:T(512)S(1)} %bitcast.128, f32[2048]{0:T(1024)S(1)} %get-tuple-element.896, ...), kind=kOutput, calls=%fused_computation.43.clone.1 | convolution fusion | flops 282066944 | bytes 827396 | tf_op jit(solution)/shard_map/while/body/eval_jaxpr/dot_general | solution.py:50
  116.8 4.5 %convolution_add_fusion.8 = f32[2048,128]{1,0:T(8,128)} fusion(f32[2048,128]{1,0:T(8,128)} %get-tuple-element.874, f32[2048]{0:T(1024)S(1)} %get-tuple-element.898, f32[512]{0:T(512)S(1)} %bitcast.129, f32[2048]{0:T(1024)S(1)} %get-tuple-element.896, f32[512]{0:T(512)S(1)} %bitcast.131, f32[2048]{0:T(1024)S(1)} %get-tuple-element.894, ...), kind=kOutput, calls=%fused_computation.41.clone.1 | convolution fusion | flops 282591232 | bytes 2269697 | tf_op jit(solution)/shard_map/while/body/eval_jaxpr/dot_general | solution.py:52
  121.2 1.1 collective-permute-start.14
  122.4 1.0 broadcast.51.clone.3
  123.4 15.3 %while.49 = (s32[]{:T(128)}, f32[4,512,128]{2,1,0:T(8,128)}, f32[4,512]{1,0:T(4,128)S(1)}, f32[2048]{0:T(1024)S(1)}, f32[4,512]{1,0:T(4,128)S(1)}, /*index=5*/f3...) while((s32[]{:T(128)}, f32[4,512,128]{2,1,0:T(8,128)}, ...), condition=%wide.region_1.2_spmd, body=%wide.region_0.1_spmd.sunk | while | flops 282066944 | bytes 844413 | solution.py:58
  123.4 3.8 %fusion.49 = f32[4,512,128]{2,1,0:T(8,128)} fusion(f32[4,512,128]{2,1,0:T(8,128)} %get-tuple-element.1006, s32[]{:T(128)} %get-tuple-element.1005, bf16[2048,128]{1,0:T(8,128)(2,1)} %get-tuple-element.1027, f32[2048]{0:T(1024)S(1)} %get-tuple-element.1026, f32[512]{0:T(512)S(1)} %bitcast.144, f32[2048]{0:T(1024)S(1)} %get-tuple-element.1024, ...), kind=kOutput, calls=%fused_computation.3.clone.1 | convolution fusion | flops 282066944 | bytes 827904 | tf_op jit(solution)/shard_map/while/body/eval_jaxpr/dot_general | solution.py:50
  127.2 3.8 %fusion.49 = f32[4,512,128]{2,1,0:T(8,128)} fusion(f32[4,512,128]{2,1,0:T(8,128)} %get-tuple-element.1006, s32[]{:T(128)} %get-tuple-element.1005, bf16[2048,128]{1,0:T(8,128)(2,1)} %get-tuple-element.1027, f32[2048]{0:T(1024)S(1)} %get-tuple-element.1026, f32[512]{0:T(512)S(1)} %bitcast.144, f32[2048]{0:T(1024)S(1)} %get-tuple-element.1024, ...), kind=kOutput, calls=%fused_computation.3.clone.1 | convolution fusion | flops 282066944 | bytes 827904 | tf_op jit(solution)/shard_map/while/body/eval_jaxpr/dot_general | solution.py:50
  131.1 3.8 %fusion.49 = f32[4,512,128]{2,1,0:T(8,128)} fusion(f32[4,512,128]{2,1,0:T(8,128)} %get-tuple-element.1006, s32[]{:T(128)} %get-tuple-element.1005, bf16[2048,128]{1,0:T(8,128)(2,1)} %get-tuple-element.1027, f32[2048]{0:T(1024)S(1)} %get-tuple-element.1026, f32[512]{0:T(512)S(1)} %bitcast.144, f32[2048]{0:T(1024)S(1)} %get-tuple-element.1024, ...), kind=kOutput, calls=%fused_computation.3.clone.1 | convolution fusion | flops 282066944 | bytes 827904 | tf_op jit(solution)/shard_map/while/body/eval_jaxpr/dot_general | solution.py:50
  134.9 3.8 %fusion.49 = f32[4,512,128]{2,1,0:T(8,128)} fusion(f32[4,512,128]{2,1,0:T(8,128)} %get-tuple-element.1006, s32[]{:T(128)} %get-tuple-element.1005, bf16[2048,128]{1,0:T(8,128)(2,1)} %get-tuple-element.1027, f32[2048]{0:T(1024)S(1)} %get-tuple-element.1026, f32[512]{0:T(512)S(1)} %bitcast.144, f32[2048]{0:T(1024)S(1)} %get-tuple-element.1024, ...), kind=kOutput, calls=%fused_computation.3.clone.1 | convolution fusion | flops 282066944 | bytes 827904 | tf_op jit(solution)/shard_map/while/body/eval_jaxpr/dot_general | solution.py:50
  138.7 1.3 add.80
  140.0 5.0 %collective-permute-done.14 = f32[2048,128]{1,0:T(8,128)} collective-permute-done((f32[2048,128]{1,0:T(8,128)}, f32[2048,128]{1,0:T(8,128)}, u32[]{:S(2)}, u32[]{:S(2)}) %collective-permute-start.14) | collective-permute-done | bytes 1048608 | tf_op jit(solution)/shard_map/ppermute | solution.py:14
  145.1 2.2 fusion.29
  147.3 3.2 %convolution_bitcast_fusion.3 = f32[256,128]{0,1:T(8,128)} fusion(f32[2048,128]{1,0:T(8,128)S(1)} %fusion.29, bf16[2048,256]{1,0:T(8,128)(2,1)} %all-gather.2.cloned.1.call-done), kind=kOutput, calls=%fused_computation.55 | convolution fusion | flops 805306368 | bytes 2228224 | tf_op jit(solution)/shard_map/dot_general | solution.py:81
  150.6 90.1 %all-reduce.2.cloned.1.call-done = f32[256,128]{0,1:T(8,128)} async-done(((f32[256,128]{0,1:T(8,128)}), f32[256,128]{0,1:T(8,128)}) %all-reduce.2.cloned.1.call-update) | async-done | bytes 131088 | tf_op jit(solution)/shard_map/psum | solution.py:82
  240.8 0.9 broadcast_multiply_fusion
  241.7 0.8 copy.6
  (70 shorter events, 0.8 us)
Async XLA Ops:
  7.2 140.2 %all-gather.2.cloned.1.call-start = ((), (), s32[]{:S(2)}) async-start(), calls=%async_computation | async-start | bytes 1572864 | tf_op jit(solution)/shard_map/all_gather | solution.py:65
  7.2 9.7 %collective-permute-start.2 = (bf16[2048]{0:T(1024)(128)(2,1)}, bf16[2048]{0:T(1024)(128)(2,1)S(1)}, u32[]{:S(2)}, u32[]{:S(2)}) collective-permute-start(bf16[2048]{0:T(1024)(128)(2,1)} %param.14), channel_id=1, source_target_pairs={{0,2},{2,4},{4,6},{6,8},{8,10},{10,12},{12,14},{14,16},{16,18},{18... | collective-permute-start | bytes 12296 | tf_op jit(solution)/shard_map/ppermute | solution.py:14
  7.7 14.2 %collective-permute-start.7 = (bf16[2048]{0:T(1024)(128)(2,1)}, bf16[2048]{0:T(1024)(128)(2,1)S(1)}, u32[]{:S(2)}, u32[]{:S(2)}) collective-permute-start(bf16[2048]{0:T(1024)(128)(2,1)} %param.14), channel_id=1, source_target_pairs={{0,4},{2,6},{4,8},{6,10},{8,12},{10,14},{12,16},{14,18},{16,20},{1... | collective-permute-start | bytes 12296 | tf_op jit(solution)/shard_map/ppermute | solution.py:14
  10.3 19.2 %collective-permute-start.3 = (bf16[2048,128]{1,0:T(8,128)(2,1)}, bf16[2048,128]{1,0:T(8,128)(2,1)S(1)}, u32[]{:S(2)}, u32[]{:S(2)}) collective-permute-start(bf16[2048,128]{1,0:T(8,128)(2,1)} %param.12), channel_id=1, source_target_pairs={{0,2},{2,4},{4,6},{6,8},{8,10},{10,12},{12,14},{14,16},{16,18},{18... | collective-permute-start | bytes 1572872 | tf_op jit(solution)/shard_map/ppermute | solution.py:14
  11.6 229.1 %all-reduce.2.cloned.1.call-start = ((), (), s32[]{:S(2)}) async-start(), calls=%async_computation.1 | async-start | bytes 262144 | tf_op jit(solution)/shard_map/psum | solution.py:82
  11.7 10.2 %collective-permute-start = (bf16[2048]{0:T(1024)(128)(2,1)}, bf16[2048]{0:T(1024)(128)(2,1)S(1)}, u32[]{:S(2)}, u32[]{:S(2)}) collective-permute-start(bf16[2048]{0:T(1024)(128)(2,1)} %param.15), channel_id=1, source_target_pairs={{0,2},{2,4},{4,6},{6,8},{8,10},{10,12},{12,14},{14,16},{16,18},{18... | collective-permute-start | bytes 12296 | tf_op jit(solution)/shard_map/ppermute | solution.py:14
  12.1 9.8 %collective-permute-start.1 = (bf16[2048]{0:T(1024)(128)(2,1)}, bf16[2048]{0:T(1024)(128)(2,1)S(1)}, u32[]{:S(2)}, u32[]{:S(2)}) collective-permute-start(bf16[2048]{0:T(1024)(128)(2,1)} %param.13), channel_id=1, source_target_pairs={{0,2},{2,4},{4,6},{6,8},{8,10},{10,12},{12,14},{14,16},{16,18},{18... | collective-permute-start | bytes 12296 | tf_op jit(solution)/shard_map/ppermute | solution.py:14
  16.9 7.5 %collective-permute-start.5 = (bf16[2048]{0:T(1024)(128)(2,1)}, bf16[2048]{0:T(1024)(128)(2,1)S(1)}, u32[]{:S(2)}, u32[]{:S(2)}) collective-permute-start(bf16[2048]{0:T(1024)(128)(2,1)} %param.15), channel_id=1, source_target_pairs={{0,4},{2,6},{4,8},{6,10},{8,12},{10,14},{12,16},{14,18},{16,20},{1... | collective-permute-start | bytes 12296 | tf_op jit(solution)/shard_map/ppermute | solution.py:14
  21.9 6.5 %collective-permute-start.6 = (bf16[2048]{0:T(1024)(128)(2,1)}, bf16[2048]{0:T(1024)(128)(2,1)S(1)}, u32[]{:S(2)}, u32[]{:S(2)}) collective-permute-start(bf16[2048]{0:T(1024)(128)(2,1)} %param.13), channel_id=1, source_target_pairs={{0,4},{2,6},{4,8},{6,10},{8,12},{10,14},{12,16},{14,18},{16,20},{1... | collective-permute-start | bytes 12296 | tf_op jit(solution)/shard_map/ppermute | solution.py:14
  21.9 7.6 %collective-permute-start.12 = (bf16[2048]{0:T(1024)(128)(2,1)}, bf16[2048]{0:T(1024)(128)(2,1)S(1)}, u32[]{:S(2)}, u32[]{:S(2)}) collective-permute-start(bf16[2048]{0:T(1024)(128)(2,1)} %param.14), channel_id=1, source_target_pairs={{0,6},{2,8},{4,10},{6,12},{8,14},{10,16},{12,18},{14,20},{16,22},{... | collective-permute-start | bytes 12296 | tf_op jit(solution)/shard_map/ppermute | solution.py:14
  21.9 6.5 %collective-permute-start.10 = (bf16[2048]{0:T(1024)(128)(2,1)}, bf16[2048]{0:T(1024)(128)(2,1)S(1)}, u32[]{:S(2)}, u32[]{:S(2)}) collective-permute-start(bf16[2048]{0:T(1024)(128)(2,1)} %param.15), channel_id=1, source_target_pairs={{0,6},{2,8},{4,10},{6,12},{8,14},{10,16},{12,18},{14,20},{16,22},{... | collective-permute-start | bytes 12296 | tf_op jit(solution)/shard_map/ppermute | solution.py:14
  24.4 5.0 %collective-permute-start.11 = (bf16[2048]{0:T(1024)(128)(2,1)}, bf16[2048]{0:T(1024)(128)(2,1)S(1)}, u32[]{:S(2)}, u32[]{:S(2)}) collective-permute-start(bf16[2048]{0:T(1024)(128)(2,1)} %param.13), channel_id=1, source_target_pairs={{0,6},{2,8},{4,10},{6,12},{8,14},{10,16},{12,18},{14,20},{16,22},{... | collective-permute-start | bytes 12296 | tf_op jit(solution)/shard_map/ppermute | solution.py:14
  28.4 28.9 %collective-permute-start.8 = (bf16[2048,128]{1,0:T(8,128)(2,1)}, bf16[2048,128]{1,0:T(8,128)(2,1)S(1)}, u32[]{:S(2)}, u32[]{:S(2)}) collective-permute-start(bf16[2048,128]{1,0:T(8,128)(2,1)} %param.12), channel_id=1, source_target_pairs={{0,4},{2,6},{4,8},{6,10},{8,12},{10,14},{12,16},{14,18},{16,20},{1... | collective-permute-start | bytes 1572872 | tf_op jit(solution)/shard_map/ppermute | solution.py:14
  28.4 62.0 %collective-permute-start.13 = (bf16[2048,128]{1,0:T(8,128)(2,1)}, bf16[2048,128]{1,0:T(8,128)(2,1)S(1)}, u32[]{:S(2)}, u32[]{:S(2)}) collective-permute-start(bf16[2048,128]{1,0:T(8,128)(2,1)} %param.12), channel_id=1, source_target_pairs={{0,6},{2,8},{4,10},{6,12},{8,14},{10,16},{12,18},{14,20},{16,22},{... | collective-permute-start | bytes 1572872 | tf_op jit(solution)/shard_map/ppermute | solution.py:14
  55.5 84.5 %collective-permute-start.4 = (f32[2048,128]{1,0:T(8,128)}, f32[2048,128]{1,0:T(8,128)}, u32[]{:S(2)}, u32[]{:S(2)}) collective-permute-start(f32[2048,128]{1,0:T(8,128)} %get-tuple-element.265), channel_id=1, source_target_pairs={{0,30},{2,0},{4,2},{6,4},{8,6},{10,8},{12,10},{14,12},{16,14},{18,... | collective-permute-start | bytes 3145736 | tf_op jit(solution)/shard_map/ppermute | solution.py:14
  57.2 0.8 copy-start.2
  88.1 51.9 %collective-permute-start.9 = (f32[2048,128]{1,0:T(8,128)}, f32[2048,128]{1,0:T(8,128)}, u32[]{:S(2)}, u32[]{:S(2)}) collective-permute-start(f32[2048,128]{1,0:T(8,128)} %get-tuple-element.267), channel_id=1, source_target_pairs={{0,28},{2,30},{4,0},{6,2},{8,4},{10,6},{12,8},{14,10},{16,12},{18,... | collective-permute-start | bytes 3145736 | tf_op jit(solution)/shard_map/ppermute | solution.py:14
  90.4 0.8 copy-start.1
  121.2 23.8 %collective-permute-start.14 = (f32[2048,128]{1,0:T(8,128)}, f32[2048,128]{1,0:T(8,128)}, u32[]{:S(2)}, u32[]{:S(2)}) collective-permute-start(f32[2048,128]{1,0:T(8,128)} %get-tuple-element.269), channel_id=1, source_target_pairs={{0,26},{2,28},{4,30},{6,0},{8,2},{10,4},{12,6},{14,8},{16,10},{18,... | collective-permute-start | bytes 3145736 | tf_op jit(solution)/shard_map/ppermute | solution.py:14
  147.3 3.3 %copy-start = (f32[2048,128]{1,0:T(8,128)}, f32[2048,128]{1,0:T(8,128)S(1)}, u32[]{:S(2)}) copy-start(f32[2048,128]{1,0:T(8,128)S(1)} %fusion.29) | copy-start | bytes 3145732
Sparse Core Ops, SparseCore 0:
  11.7 21.7 all-gather.1
  150.7 89.9 all-reduce.1
where the time goes:
time: 252 us; the launch traced here: 249 us
  matrix products  104 us (41%)
  waiting for transfers between devices  103 us (41%)
  starting transfers between devices  16.1 us (6%)
  between operations  14.2 us (6%)
  other arithmetic  6.77 us (3%)
  local copies, waits for them, and re-layouts  5.33 us (2%)
    psum x1, waiting for transfers between devices, shards(): gram = lax.psum(partial_value, 'blk') / (count * lax.axis_size('blk'))  90.1 us
    dot_general x12, matrix products, step_fn(): lax.dot_general(values, row_dirs, (((0,), (0,)), ((), ())), preferred_ele...  52.7 us
    dot_general x16, matrix products, step_fn(): forward = jnp.dot(values, other_dirs, preferred_element_type=jnp.float32)  47.7 us
    ppermute x15, starting transfers between devices, shifted(): return lax.ppermute(value, axis, pairs)  16 us
    ppermute x15, waiting for transfers between devices, shifted(): return lax.ppermute(value, axis, pairs)  12.7 us
  transfers between devices with their start and end apart: 17, of which 5 were waited for; matrix products, arithmetic and copies ran while one was open for 44% of the time, Pallas kernels for 0%

commit v1 on v0

v1 whole, which is shorter than its diff:
```python
import functools

import jax
import jax.numpy as jnp
from jax import lax
from jax.experimental import pallas as pl
from jax.experimental.pallas import tpu as pltpu
from jax.sharding import PartitionSpec as P

MESH = pl.DeviceIdType.MESH
ROW_STEP = 512
COL_STEP = 256
MIDDLE = 4.0
SOFTEN = 0.01
PIECES = 16
SLOTS = 7


def split_three(value):
    high = value.astype(jnp.bfloat16).astype(jnp.float32)
    rest = value - high
    mid = rest.astype(jnp.bfloat16).astype(jnp.float32)
    return high, mid, rest - mid


def panel_kernel(
    n, dirs_ref, geom_ref, product_ref, gram_ref,
    dirs, other, pieces, rows, flat,
    send_dirs, recv_dirs, send_geom, recv_geom, send_other, recv_other,
):
    me = lax.axis_index("blk")
    half = lax.axis_index("rhs")
    count = dirs_ref.shape[0]
    width = dirs_ref.shape[1]
    sign = 1 - 2 * lax.rem(me, 2)

    def block(offset):
        return lax.rem(me + offset * sign + n, n)

    pair = block(1)

    barrier = pltpu.get_barrier_semaphore()
    for offset in (1, -1, 2, -2, 3, -3):
        pl.semaphore_signal(barrier, inc=1, device_id=(block(offset), half), device_id_type=MESH)
    pl.semaphore_signal(barrier, inc=1, device_id=(me, 1 - half), device_id_type=MESH)
    pl.semaphore_wait(barrier, 7)

    targets = ((1, pair), (2, block(-1)), (3, block(2)), (6, block(-3)))

    def dirs_copy(source, slot, target):
        return pltpu.make_async_remote_copy(
            src_ref=source, dst_ref=dirs.at[slot], send_sem=send_dirs.at[slot], recv_sem=recv_dirs.at[slot],
            device_id=(target, half), device_id_type=MESH)

    def geom_copy(source, slot, target):
        return pltpu.make_async_remote_copy(
            src_ref=source, dst_ref=pieces.at[slot], send_sem=send_geom.at[slot], recv_sem=recv_geom.at[slot],
            device_id=(target, half), device_id_type=MESH)

    for slot, target in targets:
        dirs_copy(dirs_ref, slot, target).start()
    across = pltpu.make_async_remote_copy(
        src_ref=dirs_ref, dst_ref=other, send_sem=send_other, recv_sem=recv_other,
        device_id=(me, 1 - half), device_id_type=MESH)
    across.start()

    axial = geom_ref[0:1, :] - MIDDLE
    cosine = geom_ref[1:2, :]
    sine = geom_ref[2:3, :]
    weight = geom_ref[3:4, :]
    scale = 1.0 / (weight * weight)
    norm = axial * axial + cosine * cosine + sine * sine + 0.5 * SOFTEN
    col_parts = (scale, norm * scale, axial * scale, cosine * scale, sine * scale)
    row_scale = scale * float(count)
    row_parts = (norm * row_scale, row_scale, -2.0 * axial * row_scale, -2.0 * cosine * row_scale,
                 -2.0 * sine * row_scale)
    flat[...] = jnp.zeros_like(flat)
    for at, part in enumerate(col_parts):
        for level, piece in enumerate(split_three(part)):
            flat[3 * at + level:3 * at + level + 1, :] = piece
    pieces[0] = flat[0:PIECES, :].astype(jnp.bfloat16)
    for slot, target in targets:
        geom_copy(pieces.at[0], slot, target).start()
    dirs[0] = dirs_ref[...]

    flat[...] = jnp.zeros_like(flat)
    for at, part in enumerate(row_parts):
        for level, piece in enumerate(split_three(part)):
            for spot in range(3):
                place = PIECES * level + 3 * at + spot
                flat[place:place + 1, :] = piece
    for start in range(0, count, 128):
        turned = flat[:, start:start + 128].T
        rows[start:start + 128, :] = turned[:, :3 * PIECES].astype(jnp.bfloat16)
    product_ref[...] = jnp.zeros_like(product_ref)

    def tile(slot):
        def step(at, carry):
            here = pl.ds(pl.multiple_of(at * ROW_STEP, ROW_STEP), ROW_STEP)
            row_feature = rows[here, :]
            total = product_ref[here, :]
            for start in range(0, count, COL_STEP):
                part = pieces[slot, :, start:start + COL_STEP]
                col_feature = jnp.concatenate([part, part, part], axis=0)
                square = jnp.dot(row_feature, col_feature, preferred_element_type=jnp.float32)
                values = lax.rsqrt(square).astype(jnp.bfloat16)
                total = total + jnp.dot(
                    values, dirs[slot, start:start + COL_STEP, :], preferred_element_type=jnp.float32)
            product_ref[here, :] = total
            return carry

        lax.fori_loop(0, count // ROW_STEP, step, 0)

    def turn(slot, carry):
        @pl.when(slot > 0)
        def _():
            dirs_copy(dirs_ref, slot, pair).wait_recv()
            geom_copy(pieces.at[0], slot, pair).wait_recv()

        @pl.when((slot == 2) | (slot == 3))
        def _():
            dirs_copy(dirs.at[slot], slot + 2, pair).start()
            geom_copy(pieces.at[slot], slot + 2, pair).start()

        tile(slot)
        return carry

    lax.fori_loop(0, SLOTS, turn, 0)

    across.wait()
    total = product_ref[...]
    high = total.astype(jnp.bfloat16)
    low = (total - high.astype(jnp.float32)).astype(jnp.bfloat16)
    inverse = 1.0 / (count * n)
    for place, value in ((half, dirs[0]), (1 - half, other[...])):
        turned = value.T
        inner = jnp.dot(turned, high, preferred_element_type=jnp.float32)
        inner = inner + jnp.dot(turned, low, preferred_element_type=jnp.float32)
        gram_ref[pl.ds(pl.multiple_of(place * width, width), width), :] = inner * inverse

    for slot in range(1, SLOTS):
        dirs_copy(dirs_ref, slot, pair).wait_send()
        geom_copy(pieces.at[0], slot, pair).wait_send()


def shards(n, directions, axial_pos, azimuth, panel_area):
    count, width = directions.shape
    angle = azimuth.astype(jnp.float32)
    geom = jnp.stack([axial_pos.astype(jnp.float32), jnp.cos(angle), jnp.sin(angle), panel_area.astype(jnp.float32)])
    vmem = pl.BlockSpec(memory_space=pltpu.VMEM)
    product, gram = pl.pallas_call(
        functools.partial(panel_kernel, n),
        out_shape=(
            jax.ShapeDtypeStruct((count, width), jnp.float32),
            jax.ShapeDtypeStruct((2 * width, width), jnp.float32),
        ),
        in_specs=[vmem, vmem],
        out_specs=(vmem, vmem),
        scratch_shapes=[
            pltpu.VMEM((SLOTS, count, width), jnp.bfloat16),
            pltpu.VMEM((count, width), jnp.bfloat16),
            pltpu.VMEM((SLOTS, PIECES, count), jnp.bfloat16),
            pltpu.VMEM((count, 3 * PIECES), jnp.bfloat16),
            pltpu.VMEM((128, count), jnp.float32),
            pltpu.SemaphoreType.DMA((SLOTS,)),
            pltpu.SemaphoreType.DMA((SLOTS,)),
            pltpu.SemaphoreType.DMA((SLOTS,)),
            pltpu.SemaphoreType.DMA((SLOTS,)),
            pltpu.SemaphoreType.DMA,
            pltpu.SemaphoreType.DMA,
        ],
        compiler_params=pltpu.CompilerParams(
            collective_id=0, has_side_effects=True, vmem_limit_bytes=48 * 1024 * 1024),
        cost_estimate=pl.CostEstimate(
            flops=SLOTS * 2 * count * count * (width + 48), bytes_accessed=4 * count * width,
            transcendentals=SLOTS * count * count),
        name="panels",
    )(directions, geom)
    return product, lax.psum(gram, "blk")


def solution(mesh):
    in_specs = (P("blk", "rhs"), P("blk"), P("blk"), P("blk"))
    out_specs = (P("blk", "rhs"), P(None, "rhs"))
    body = functools.partial(shards, mesh.shape["blk"])
    return jax.shard_map(body, mesh=mesh, in_specs=in_specs, out_specs=out_specs, check_vma=False)
```

time: 252 us -> 168 us (0.67)
  matrix products: 104 us -> 0 us
  Pallas kernels: 0 us -> 59.6 us
  starting transfers between devices: 16.1 us -> 0.04 us
  waiting for transfers between devices: 103 us -> 88.7 us
  other arithmetic: 6.77 us -> 0.78 us
    dot_general x29 -> x0, matrix products: 104 us -> none  [the longest x12 52.7 us: step_fn(): lax.dot_general(values, row_dirs, (((0,), (0,)), ((), ())), preferred_ele...]
    pallas_call x0 -> x1, Pallas kernels: none -> 59.6 us  [shards(): pl.pallas_call(functools.partial(panel_kernel, n), out_shape=(jax.ShapeDt...]
    ppermute x15 -> x0, starting transfers between devices: 16 us -> none  [shifted(): return lax.ppermute(value, axis, pairs)]
    ppermute x15 -> x0, waiting for transfers between devices: 12.7 us -> none  [shifted(): return lax.ppermute(value, axis, pairs)]
    add x2 -> x0, other arithmetic: 3.58 us -> none  [the longest x1 2.25 us: shards(): product = product + shifted(backward, 'blk', -shift_by)]
  transfers between devices with their start and end apart: 17 -> 1, of which waited for: 5 -> 1; matrix products, arithmetic and copies ran while one was open for 44% -> 0% of each run, Pallas kernels for 0% -> 0%
where the time goes in v1:
time: 168 us; the launch traced here: 167 us
  waiting for transfers between devices  88.7 us (53%)
  Pallas kernels  59.6 us (35%)
  between operations  14.1 us (8%)
  local copies, waits for them, and re-layouts  3.4 us (2%)
    psum x1, waiting for transfers between devices, shards(): return (product, lax.psum(gram, 'blk'))  88.7 us
    pallas_call x1, Pallas kernels, shards(): pl.pallas_call(functools.partial(panel_kernel, n), out_shape=(jax.ShapeDt...  59.6 us
    unnamed x10, local copies, waits for them, and re-layouts  3.4 us
  transfers between devices with their start and end apart: 1, of which 1 were waited for; matrix products, arithmetic and copies ran while one was open for 0% of the time, Pallas kernels for 0%

profile of v1, /device:TPU:0, one launch (start us, length us, event | category | flops | bytes accessed | tf_op | source)
XLA Modules:
  0.0 166.5 jit_solution(642760002476876815)
XLA Ops:
  7.2 0.0 copy-start.2
  7.2 0.0 all-reduce.2.cloned.1.call-start
  7.2 0.7 stack.28
  7.9 0.0 copy-done.2
  7.9 0.0 copy-start.3
  7.9 0.7 copy-done.3
  8.7 0.0 copy-start
  8.7 1.0 copy-done
  9.7 59.6 %panels.1 = (f32[2048,128]{1,0:T(8,128)S(1)}, f32[256,128]{1,0:T(8,128)}) custom-call(bf16[2048,128]{1,0:T(8,128)(2,1)S(1)} %copy-done, f32[4,2048]{1,0:T(4,128)S(1)} %pad_maximum_fusion.geom_ref), custom_call_target="tpu_custom_call" | custom-call | flops 10334765056 | bytes 1048576 | tf_op jit(solution)/shard_map/panels/pallas_call | solution.py:151
  69.3 0.0 all-reduce.2.cloned.1.call-update
  69.3 88.7 %all-reduce.2.cloned.1.call-done = f32[256,128]{1,0:T(8,128)} async-done(((f32[256,128]{1,0:T(8,128)}), f32[256,128]{1,0:T(8,128)}) %all-reduce.2.cloned.1.call-update) | async-done | bytes 131088 | tf_op jit(solution)/shard_map/psum | solution.py:179
  158.0 0.0 copy-start.1
  158.0 1.0 copy.9
  159.0 0.1 copy-done.1
  159.0 0.7 copy.10
  (3 shorter events, 0.1 us)
Async XLA Ops:
  7.2 0.7 copy-start.2
  7.2 150.8 %all-reduce.2.cloned.1.call-start = ((), (), s32[]{:S(2)}) async-start(), calls=%async_computation | async-start | bytes 262144 | tf_op jit(solution)/shard_map/psum | solution.py:179
  7.9 0.7 copy-start.3
  8.7 1.0 copy-start
  158.0 1.0 copy-start.1
Sparse Core Ops, SparseCore 0:
  69.4 88.5 all-reduce.1

commit v2 on v1

--- a/solution.py
+++ b/solution.py
@@ -9,7 +9,7 @@
 
 MESH = pl.DeviceIdType.MESH
 ROW_STEP = 512
-COL_STEP = 256
+COL_STEP = 512
 MIDDLE = 4.0
 SOFTEN = 0.01
 PIECES = 16
@@ -24,9 +24,10 @@
 
 
 def panel_kernel(
-    n, dirs_ref, geom_ref, product_ref, gram_ref,
-    dirs, other, pieces, rows, flat,
+    n, reduce_here, dirs_ref, geom_ref, product_ref, gram_ref,
+    dirs, other, pieces, rows, flat, partial, landed, summed,
     send_dirs, recv_dirs, send_geom, recv_geom, send_other, recv_other,
+    send_part, recv_part, send_sum, recv_sum,
 ):
     me = lax.axis_index("blk")
     half = lax.axis_index("rhs")
@@ -40,10 +41,18 @@
     pair = block(1)
 
     barrier = pltpu.get_barrier_semaphore()
-    for offset in (1, -1, 2, -2, 3, -3):
-        pl.semaphore_signal(barrier, inc=1, device_id=(block(offset), half), device_id_type=MESH)
     pl.semaphore_signal(barrier, inc=1, device_id=(me, 1 - half), device_id_type=MESH)
-    pl.semaphore_wait(barrier, 7)
+    if reduce_here:
+        def greet(step, carry):
+            pl.semaphore_signal(barrier, inc=1, device_id=(lax.rem(me + step, n), half), device_id_type=MESH)
+            return carry
+
+        lax.fori_loop(1, n, greet, 0)
+        pl.semaphore_wait(barrier, n)
+    else:
+        for offset in (1, -1, 2, -2, 3, -3):
+            pl.semaphore_signal(barrier, inc=1, device_id=(block(offset), half), device_id_type=MESH)
+        pl.semaphore_wait(barrier, 7)
 
     targets = ((1, pair), (2, block(-1)), (3, block(2)), (6, block(-3)))
 
@@ -99,13 +108,18 @@
             here = pl.ds(pl.multiple_of(at * ROW_STEP, ROW_STEP), ROW_STEP)
             row_feature = rows[here, :]
             total = product_ref[here, :]
-            for start in range(0, count, COL_STEP):
+            def squares(start):
                 part = pieces[slot, :, start:start + COL_STEP]
                 col_feature = jnp.concatenate([part, part, part], axis=0)
-                square = jnp.dot(row_feature, col_feature, preferred_element_type=jnp.float32)
+                return jnp.dot(row_feature, col_feature, preferred_element_type=jnp.float32)
+
+            square = squares(0)
+            for start in range(0, count, COL_STEP):
+                ahead = squares(start + COL_STEP) if start + COL_STEP < count else None
                 values = lax.rsqrt(square).astype(jnp.bfloat16)
                 total = total + jnp.dot(
                     values, dirs[slot, start:start + COL_STEP, :], preferred_element_type=jnp.float32)
+                square = ahead
             product_ref[here, :] = total
             return carry
 
@@ -136,7 +150,46 @@
         turned = value.T
         inner = jnp.dot(turned, high, preferred_element_type=jnp.float32)
         inner = inner + jnp.dot(turned, low, preferred_element_type=jnp.float32)
-        gram_ref[pl.ds(pl.multiple_of(place * width, width), width), :] = inner * inverse
+        partial[pl.ds(pl.multiple_of(place * width, width), width), :] = inner * inverse
+
+    if reduce_here:
+        depth = landed.shape[1]
+
+        def rows_of(owner):
+            return pl.ds(pl.multiple_of(owner * depth, depth), depth)
+
+        def part_copy(step):
+            target = lax.rem(me + step, n)
+            return pltpu.make_async_remote_copy(
+                src_ref=partial.at[rows_of(target)], dst_ref=landed.at[step],
+                send_sem=send_part.at[step], recv_sem=recv_part.at[step],
+                device_id=(target, half), device_id_type=MESH)
+
+        def sum_copy(step):
+            target = lax.rem(me + step, n)
+            return pltpu.make_async_remote_copy(
+                src_ref=summed.at[rows_of(me)], dst_ref=summed.at[rows_of(me)],
+                send_sem=send_sum.at[step], recv_sem=recv_sum.at[step],
+                device_id=(target, half), device_id_type=MESH)
+
+        def each(act):
+            def run(step, carry):
+                act(step)
+                return carry
+
+            lax.fori_loop(1, n, run, 0)
+
+        each(lambda step: part_copy(step).start())
+        landed[0] = partial[rows_of(me), :]
+        each(lambda step: part_copy(step).wait_recv())
+        summed[rows_of(me), :] = jnp.sum(landed[...], axis=0)
+        each(lambda step: sum_copy(step).start())
+        each(lambda step: sum_copy(step).wait_recv())
+        gram_ref[...] = summed[...]
+        each(lambda step: part_copy(step).wait_send())
+        each(lambda step: sum_copy(step).wait_send())
+    else:
+        gram_ref[...] = partial[...]
 
     for slot in range(1, SLOTS):
         dirs_copy(dirs_ref, slot, pair).wait_send()
@@ -148,8 +201,10 @@
     angle = azimuth.astype(jnp.float32)
     geom = jnp.stack([axial_pos.astype(jnp.float32), jnp.cos(angle), jnp.sin(angle), panel_area.astype(jnp.float32)])
     vmem = pl.BlockSpec(memory_space=pltpu.VMEM)
+    reduce_here = (2 * width) % (8 * n) == 0
+    depth = 2 * width // n if reduce_here else 8
     product, gram = pl.pallas_call(
-        functools.partial(panel_kernel, n),
+        functools.partial(panel_kernel, n, reduce_here),
         out_shape=(
             jax.ShapeDtypeStruct((count, width), jnp.float32),
             jax.ShapeDtypeStruct((2 * width, width), jnp.float32),
@@ -162,12 +217,19 @@
             pltpu.VMEM((SLOTS, PIECES, count), jnp.bfloat16),
             pltpu.VMEM((count, 3 * PIECES), jnp.bfloat16),
             pltpu.VMEM((128, count), jnp.float32),
+            pltpu.VMEM((2 * width, width), jnp.float32),
+            pltpu.VMEM((n, depth, width), jnp.float32),
+            pltpu.VMEM((2 * width, width), jnp.float32),
             pltpu.SemaphoreType.DMA((SLOTS,)),
             pltpu.SemaphoreType.DMA((SLOTS,)),
             pltpu.SemaphoreType.DMA((SLOTS,)),
             pltpu.SemaphoreType.DMA((SLOTS,)),
             pltpu.SemaphoreType.DMA,
             pltpu.SemaphoreType.DMA,
+            pltpu.SemaphoreType.DMA((n,)),
+            pltpu.SemaphoreType.DMA((n,)),
+            pltpu.SemaphoreType.DMA((n,)),
+            pltpu.SemaphoreType.DMA((n,)),
         ],
         compiler_params=pltpu.CompilerParams(
             collective_id=0, has_side_effects=True, vmem_limit_bytes=48 * 1024 * 1024),
@@ -176,7 +238,7 @@
             transcendentals=SLOTS * count * count),
         name="panels",
     )(directions, geom)
-    return product, lax.psum(gram, "blk")
+    return product, gram if reduce_here else lax.psum(gram, "blk")
 
 
 def solution(mesh):

time: 168 us -> 75.9 us (0.45)
  waiting for transfers between devices: 88.7 us -> 0 us
  between operations: 14.1 us -> 0.67 us
  Pallas kernels: 59.6 us -> 70.9 us
    psum x1 -> x0, waiting for transfers between devices: 88.7 us -> none  [shards(): return (product, lax.psum(gram, 'blk'))]
    pallas_call x1, Pallas kernels: 59.6 us -> 70.9 us  [shards(): pl.pallas_call(functools.partial(panel_kernel, n, reduce_here), out_shape...]
    unnamed x10 -> x8, local copies, waits for them, and re-layouts: 3.4 us -> 3.35 us
  transfers between devices with their start and end apart: 1 -> 0, of which waited for: 1 -> 0; matrix products, arithmetic and copies ran while one was open for 0% -> 0% of each run, Pallas kernels for 0% -> 0%
where the time goes in v2:
time: 75.9 us; the launch traced here: 75.7 us
  Pallas kernels  70.9 us (93%)
  local copies, waits for them, and re-layouts  3.35 us (4%)
  other arithmetic  0.78 us (1%)
    pallas_call x1, Pallas kernels, shards(): pl.pallas_call(functools.partial(panel_kernel, n, reduce_here), out_shape...  70.9 us
    unnamed x8, local copies, waits for them, and re-layouts  3.35 us

profile of v2, /device:TPU:0, one launch (start us, length us, event | category | flops | bytes accessed | tf_op | source)
XLA Modules:
  0.0 75.7 jit_solution(13185705247007437814)
XLA Ops:
  0.6 0.0 copy-start.1
  0.6 0.7 stack.28
  1.3 0.0 copy-done.1
  1.3 0.0 copy-start.2
  1.3 0.7 copy-done.2
  2.1 0.0 copy-start
  2.1 1.0 %copy-done = bf16[2048,128]{1,0:T(8,128)(2,1)S(1)} copy-done((bf16[2048,128]{1,0:T(8,128)(2,1)S(1)}, bf16[2048,128]{1,0:T(8,128)(2,1)}, u32[]{:S(2)}) %copy-start) | copy-done | bytes 524312
  3.2 70.9 %panels.1 = (f32[2048,128]{1,0:T(8,128)S(1)}, f32[256,128]{1,0:T(8,128)S(1)}) custom-call(bf16[2048,128]{1,0:T(8,128)(2,1)S(1)} %copy-done, f32[4,2048]{1,0:T(4,128)S(1)} %pad_maximum_fusion.geom_ref), custom_call_target="tpu_custom_call" | custom-call | flops 10334765056 | bytes 1048576 | tf_op jit(solution)/shard_map/panels/pallas_call | solution.py:206
  74.0 1.0 %copy.8 = f32[2048,128]{1,0:T(8,128)} copy(f32[2048,128]{1,0:T(8,128)S(1)} %get-tuple-element.6) | data formatting | bytes 2097152
  75.0 0.7 copy.9
  (3 shorter events, 0.1 us)
Async XLA Ops:
  0.6 0.7 copy-start.1
  1.3 0.7 copy-start.2
  2.1 1.0 %copy-start = (bf16[2048,128]{1,0:T(8,128)(2,1)S(1)}, bf16[2048,128]{1,0:T(8,128)(2,1)}, u32[]{:S(2)}) copy-start(bf16[2048,128]{1,0:T(8,128)(2,1)} %dirs_ref.1) | copy-start | bytes 1572868

commit v3 on v2

--- a/solution.py
+++ b/solution.py
@@ -21,6 +21,11 @@
     rest = value - high
     mid = rest.astype(jnp.bfloat16).astype(jnp.float32)
     return high, mid, rest - mid
+
+
+def inverse_root(four_square):
+    first = lax.rsqrt(four_square.astype(jnp.bfloat16)).astype(jnp.float32)
+    return (first * (3.0 - four_square * first * first)).astype(jnp.bfloat16)
 
 
 def panel_kernel(
@@ -80,7 +85,7 @@
     scale = 1.0 / (weight * weight)
     norm = axial * axial + cosine * cosine + sine * sine + 0.5 * SOFTEN
     col_parts = (scale, norm * scale, axial * scale, cosine * scale, sine * scale)
-    row_scale = scale * float(count)
+    row_scale = scale * (4.0 * count)
     row_parts = (norm * row_scale, row_scale, -2.0 * axial * row_scale, -2.0 * cosine * row_scale,
                  -2.0 * sine * row_scale)
     flat[...] = jnp.zeros_like(flat)
@@ -116,7 +121,7 @@
             square = squares(0)
             for start in range(0, count, COL_STEP):
                 ahead = squares(start + COL_STEP) if start + COL_STEP < count else None
-                values = lax.rsqrt(square).astype(jnp.bfloat16)
+                values = inverse_root(square)
                 total = total + jnp.dot(
                     values, dirs[slot, start:start + COL_STEP, :], preferred_element_type=jnp.float32)
                 square = ahead

time: 75.9 us -> 76.7 us (1.011)
  Pallas kernels: 70.9 us -> 71.7 us
    pallas_call x1, Pallas kernels: 70.9 us -> 71.7 us  [shards(): pl.pallas_call(functools.partial(panel_kernel, n, reduce_here), out_shape...]
where the time goes in v3:
time: 76.7 us; the launch traced here: 76.5 us
  Pallas kernels  71.7 us (93%)
  local copies, waits for them, and re-layouts  3.35 us (4%)
  other arithmetic  0.78 us (1%)
    pallas_call x1, Pallas kernels, shards(): pl.pallas_call(functools.partial(panel_kernel, n, reduce_here), out_shape...  71.7 us
    unnamed x8, local copies, waits for them, and re-layouts  3.35 us

profile of v3, /device:TPU:0, one launch (start us, length us, event | category | flops | bytes accessed | tf_op | source)
XLA Modules:
  0.0 76.5 jit_solution(12172561024569635313)
XLA Ops:
  0.6 0.0 copy-start.1
  0.6 0.7 stack.28
  1.3 0.0 copy-done.1
  1.3 0.0 copy-start.2
  1.3 0.7 copy-done.2
  2.1 0.0 copy-start
  2.1 1.0 %copy-done = bf16[2048,128]{1,0:T(8,128)(2,1)S(1)} copy-done((bf16[2048,128]{1,0:T(8,128)(2,1)S(1)}, bf16[2048,128]{1,0:T(8,128)(2,1)}, u32[]{:S(2)}) %copy-start) | copy-done | bytes 524312
  3.2 71.7 %panels.1 = (f32[2048,128]{1,0:T(8,128)S(1)}, f32[256,128]{1,0:T(8,128)S(1)}) custom-call(bf16[2048,128]{1,0:T(8,128)(2,1)S(1)} %copy-done, f32[4,2048]{1,0:T(4,128)S(1)} %pad_maximum_fusion.geom_ref), custom_call_target="tpu_custom_call" | custom-call | flops 10334765056 | bytes 1048576 | tf_op jit(solution)/shard_map/panels/pallas_call | solution.py:211
  74.8 1.0 %copy.8 = f32[2048,128]{1,0:T(8,128)} copy(f32[2048,128]{1,0:T(8,128)S(1)} %get-tuple-element.6) | data formatting | bytes 2097152
  75.8 0.7 copy.9
  (3 shorter events, 0.1 us)
Async XLA Ops:
  0.6 0.7 copy-start.1
  1.3 0.7 copy-start.2
  2.1 1.0 %copy-start = (bf16[2048,128]{1,0:T(8,128)(2,1)S(1)}, bf16[2048,128]{1,0:T(8,128)(2,1)}, u32[]{:S(2)}) copy-start(bf16[2048,128]{1,0:T(8,128)(2,1)} %dirs_ref.1) | copy-start | bytes 1572868

commit v4 on v2

--- a/solution.py
+++ b/solution.py
@@ -8,24 +8,18 @@
 from jax.sharding import PartitionSpec as P
 
 MESH = pl.DeviceIdType.MESH
-ROW_STEP = 512
+ROW_STEP = 256
+SUB_STEP = 16
 COL_STEP = 512
 MIDDLE = 4.0
 SOFTEN = 0.01
-PIECES = 16
+FEATURES = 8
 SLOTS = 7
-
-
-def split_three(value):
-    high = value.astype(jnp.bfloat16).astype(jnp.float32)
-    rest = value - high
-    mid = rest.astype(jnp.bfloat16).astype(jnp.float32)
-    return high, mid, rest - mid
 
 
 def panel_kernel(
     n, reduce_here, dirs_ref, geom_ref, product_ref, gram_ref,
-    dirs, other, pieces, rows, flat, partial, landed, summed,
+    dirs, other, pieces, rows, columns, flat, partial, landed, summed,
     send_dirs, recv_dirs, send_geom, recv_geom, send_other, recv_other,
     send_part, recv_part, send_sum, recv_sum,
 ):
@@ -85,41 +79,41 @@
                  -2.0 * sine * row_scale)
     flat[...] = jnp.zeros_like(flat)
     for at, part in enumerate(col_parts):
-        for level, piece in enumerate(split_three(part)):
-            flat[3 * at + level:3 * at + level + 1, :] = piece
-    pieces[0] = flat[0:PIECES, :].astype(jnp.bfloat16)
+        flat[at:at + 1, :] = part
+    pieces[0] = flat[0:FEATURES, :]
     for slot, target in targets:
         geom_copy(pieces.at[0], slot, target).start()
     dirs[0] = dirs_ref[...]
 
-    flat[...] = jnp.zeros_like(flat)
     for at, part in enumerate(row_parts):
-        for level, piece in enumerate(split_three(part)):
-            for spot in range(3):
-                place = PIECES * level + 3 * at + spot
-                flat[place:place + 1, :] = piece
+        flat[at:at + 1, :] = part
     for start in range(0, count, 128):
         turned = flat[:, start:start + 128].T
-        rows[start:start + 128, :] = turned[:, :3 * PIECES].astype(jnp.bfloat16)
+        for at in range(len(row_parts)):
+            rows[at, start:start + 128, :] = jnp.broadcast_to(turned[:, at:at + 1], (128, 128))
     product_ref[...] = jnp.zeros_like(product_ref)
 
     def tile(slot):
+        for at in range(len(col_parts)):
+            columns[at] = jnp.broadcast_to(pieces[slot, at:at + 1, :], (SUB_STEP, count))
+
         def step(at, carry):
-            here = pl.ds(pl.multiple_of(at * ROW_STEP, ROW_STEP), ROW_STEP)
-            row_feature = rows[here, :]
+            base = pl.multiple_of(at * ROW_STEP, ROW_STEP)
+            here = pl.ds(base, ROW_STEP)
             total = product_ref[here, :]
-            def squares(start):
-                part = pieces[slot, :, start:start + COL_STEP]
-                col_feature = jnp.concatenate([part, part, part], axis=0)
-                return jnp.dot(row_feature, col_feature, preferred_element_type=jnp.float32)
-
-            square = squares(0)
             for start in range(0, count, COL_STEP):
-                ahead = squares(start + COL_STEP) if start + COL_STEP < count else None
-                values = lax.rsqrt(square).astype(jnp.bfloat16)
+                strips = []
+                for sub in range(0, ROW_STEP, SUB_STEP):
+                    square = None
+                    for part in range(len(col_parts)):
+                        row = rows[part, pl.ds(pl.multiple_of(base + sub, SUB_STEP), SUB_STEP), :]
+                        row = jnp.concatenate([row] * (COL_STEP // 128), axis=1)
+                        term = row * columns[part, :, start:start + COL_STEP]
+                        square = term if square is None else square + term
+                    strips.append(lax.rsqrt(square).astype(jnp.bfloat16))
+                values = jnp.concatenate(strips, axis=0)
                 total = total + jnp.dot(
                     values, dirs[slot, start:start + COL_STEP, :], preferred_element_type=jnp.float32)
-                square = ahead
             product_ref[here, :] = total
             return carry
 
@@ -214,8 +208,9 @@
         scratch_shapes=[
             pltpu.VMEM((SLOTS, count, width), jnp.bfloat16),
             pltpu.VMEM((count, width), jnp.bfloat16),
-            pltpu.VMEM((SLOTS, PIECES, count), jnp.bfloat16),
-            pltpu.VMEM((count, 3 * PIECES), jnp.bfloat16),
+            pltpu.VMEM((SLOTS, FEATURES, count), jnp.float32),
+            pltpu.VMEM((5, count, 128), jnp.float32),
+            pltpu.VMEM((5, SUB_STEP, count), jnp.float32),
             pltpu.VMEM((128, count), jnp.float32),
             pltpu.VMEM((2 * width, width), jnp.float32),
             pltpu.VMEM((n, depth, width), jnp.float32),
@@ -234,7 +229,7 @@
         compiler_params=pltpu.CompilerParams(
             collective_id=0, has_side_effects=True, vmem_limit_bytes=48 * 1024 * 1024),
         cost_estimate=pl.CostEstimate(
-            flops=SLOTS * 2 * count * count * (width + 48), bytes_accessed=4 * count * width,
+            flops=SLOTS * 2 * count * count * (width + 9), bytes_accessed=4 * count * width,
             transcendentals=SLOTS * count * count),
         name="panels",
     )(directions, geom)

time: 75.9 us -> 86.3 us (1.14)
  Pallas kernels: 70.9 us -> 81.3 us
    pallas_call x1, Pallas kernels: 70.9 us -> 81.3 us  [shards(): pl.pallas_call(functools.partial(panel_kernel, n, reduce_here), out_shape...]
where the time goes in v4:
time: 86.3 us; the launch traced here: 86.1 us
  Pallas kernels  81.3 us (94%)
  local copies, waits for them, and re-layouts  3.35 us (4%)
    pallas_call x1, Pallas kernels, shards(): pl.pallas_call(functools.partial(panel_kernel, n, reduce_here), out_shape...  81.3 us
    unnamed x8, local copies, waits for them, and re-layouts  3.35 us

profile of v4, /device:TPU:0, one launch (start us, length us, event | category | flops | bytes accessed | tf_op | source)
XLA Modules:
  0.0 86.1 jit_solution(11735389525111158749)
XLA Ops:
  0.6 0.0 copy-start.1
  0.6 0.7 stack.28
  1.3 0.0 copy-done.1
  1.3 0.0 copy-start.2
  1.3 0.7 copy-done.2
  2.1 0.0 copy-start
  2.1 1.0 %copy-done = bf16[2048,128]{1,0:T(8,128)(2,1)S(1)} copy-done((bf16[2048,128]{1,0:T(8,128)(2,1)S(1)}, bf16[2048,128]{1,0:T(8,128)(2,1)}, u32[]{:S(2)}) %copy-start) | copy-done | bytes 524312
  3.2 81.3 %panels.1 = (f32[2048,128]{1,0:T(8,128)S(1)}, f32[256,128]{1,0:T(8,128)S(1)}) custom-call(bf16[2048,128]{1,0:T(8,128)(2,1)S(1)} %copy-done, f32[4,2048]{1,0:T(4,128)S(1)} %pad_maximum_fusion.geom_ref), custom_call_target="tpu_custom_call" | custom-call | flops 8044675072 | bytes 1048576 | tf_op jit(solution)/shard_map/panels/pallas_call | solution.py:200
  84.5 1.0 %copy.8 = f32[2048,128]{1,0:T(8,128)} copy(f32[2048,128]{1,0:T(8,128)S(1)} %get-tuple-element.6) | data formatting | bytes 2097152
  85.4 0.7 copy.9
  (3 shorter events, 0.1 us)
Async XLA Ops:
  0.6 0.7 copy-start.1
  1.3 0.7 copy-start.2
  2.1 1.0 %copy-start = (bf16[2048,128]{1,0:T(8,128)(2,1)S(1)}, bf16[2048,128]{1,0:T(8,128)(2,1)}, u32[]{:S(2)}) copy-start(bf16[2048,128]{1,0:T(8,128)(2,1)} %dirs_ref.1) | copy-start | bytes 1572868

commit v5 on v2

--- a/solution.py
+++ b/solution.py
@@ -8,8 +8,8 @@
 from jax.sharding import PartitionSpec as P
 
 MESH = pl.DeviceIdType.MESH
-ROW_STEP = 512
-COL_STEP = 512
+COL_STEP = 256
+COL_GROUP = 1024
 MIDDLE = 4.0
 SOFTEN = 0.01
 PIECES = 16
@@ -105,25 +105,29 @@
 
     def tile(slot):
         def step(at, carry):
-            here = pl.ds(pl.multiple_of(at * ROW_STEP, ROW_STEP), ROW_STEP)
-            row_feature = rows[here, :]
-            total = product_ref[here, :]
+            base = at * COL_GROUP
+            row_feature = rows[...]
+
+            def here(start):
+                return pl.ds(pl.multiple_of(base + start, COL_STEP), COL_STEP)
+
             def squares(start):
-                part = pieces[slot, :, start:start + COL_STEP]
+                part = pieces[slot, :, here(start)]
                 col_feature = jnp.concatenate([part, part, part], axis=0)
                 return jnp.dot(row_feature, col_feature, preferred_element_type=jnp.float32)
 
+            total = product_ref[...]
             square = squares(0)
-            for start in range(0, count, COL_STEP):
-                ahead = squares(start + COL_STEP) if start + COL_STEP < count else None
+            for start in range(0, COL_GROUP, COL_STEP):
+                ahead = squares(start + COL_STEP) if start + COL_STEP < COL_GROUP else None
                 values = lax.rsqrt(square).astype(jnp.bfloat16)
                 total = total + jnp.dot(
-                    values, dirs[slot, start:start + COL_STEP, :], preferred_element_type=jnp.float32)
+                    values, dirs[slot, here(start), :], preferred_element_type=jnp.float32)
                 square = ahead
-            product_ref[here, :] = total
+            product_ref[...] = total
             return carry
 
-        lax.fori_loop(0, count // ROW_STEP, step, 0)
+        lax.fori_loop(0, count // COL_GROUP, step, 0)
 
     def turn(slot, carry):
         @pl.when(slot > 0)

time: 75.9 us -> 73.3 us (0.966)
  Pallas kernels: 70.9 us -> 68.2 us
    pallas_call x1, Pallas kernels: 70.9 us -> 68.2 us  [shards(): pl.pallas_call(functools.partial(panel_kernel, n, reduce_here), out_shape...]
where the time goes in v5:
time: 73.3 us; the launch traced here: 73.1 us
  Pallas kernels  68.2 us (93%)
  local copies, waits for them, and re-layouts  3.35 us (5%)
  other arithmetic  0.78 us (1%)
    pallas_call x1, Pallas kernels, shards(): pl.pallas_call(functools.partial(panel_kernel, n, reduce_here), out_shape...  68.2 us
    unnamed x8, local copies, waits for them, and re-layouts  3.35 us

profile of v5, /device:TPU:0, one launch (start us, length us, event | category | flops | bytes accessed | tf_op | source)
XLA Modules:
  0.0 73.1 jit_solution(5247215146040205217)
XLA Ops:
  0.6 0.0 copy-start.1
  0.6 0.7 stack.28
  1.3 0.0 copy-done.1
  1.3 0.0 copy-start.2
  1.3 0.7 copy-done.2
  2.1 0.0 copy-start
  2.1 1.0 %copy-done = bf16[2048,128]{1,0:T(8,128)(2,1)S(1)} copy-done((bf16[2048,128]{1,0:T(8,128)(2,1)S(1)}, bf16[2048,128]{1,0:T(8,128)(2,1)}, u32[]{:S(2)}) %copy-start) | copy-done | bytes 524312
  3.2 68.2 %panels.1 = (f32[2048,128]{1,0:T(8,128)S(1)}, f32[256,128]{1,0:T(8,128)S(1)}) custom-call(bf16[2048,128]{1,0:T(8,128)(2,1)S(1)} %copy-done, f32[4,2048]{1,0:T(4,128)S(1)} %pad_maximum_fusion.geom_ref), custom_call_target="tpu_custom_call" | custom-call | flops 10334765056 | bytes 1048576 | tf_op jit(solution)/shard_map/panels/pallas_call | solution.py:210
  71.4 1.0 %copy.8 = f32[2048,128]{1,0:T(8,128)} copy(f32[2048,128]{1,0:T(8,128)S(1)} %get-tuple-element.6) | data formatting | bytes 2097152
  72.4 0.7 copy.9
  (3 shorter events, 0.1 us)
Async XLA Ops:
  0.6 0.7 copy-start.1
  1.3 0.7 copy-start.2
  2.1 1.0 %copy-start = (bf16[2048,128]{1,0:T(8,128)(2,1)S(1)}, bf16[2048,128]{1,0:T(8,128)(2,1)}, u32[]{:S(2)}) copy-start(bf16[2048,128]{1,0:T(8,128)(2,1)} %dirs_ref.1) | copy-start | bytes 1572868

commit v6 on v5

--- a/solution.py
+++ b/solution.py
@@ -48,11 +48,9 @@
             return carry
 
         lax.fori_loop(1, n, greet, 0)
-        pl.semaphore_wait(barrier, n)
     else:
         for offset in (1, -1, 2, -2, 3, -3):
             pl.semaphore_signal(barrier, inc=1, device_id=(block(offset), half), device_id_type=MESH)
-        pl.semaphore_wait(barrier, 7)
 
     targets = ((1, pair), (2, block(-1)), (3, block(2)), (6, block(-3)))
 
@@ -65,13 +63,6 @@
         return pltpu.make_async_remote_copy(
             src_ref=source, dst_ref=pieces.at[slot], send_sem=send_geom.at[slot], recv_sem=recv_geom.at[slot],
             device_id=(target, half), device_id_type=MESH)
-
-    for slot, target in targets:
-        dirs_copy(dirs_ref, slot, target).start()
-    across = pltpu.make_async_remote_copy(
-        src_ref=dirs_ref, dst_ref=other, send_sem=send_other, recv_sem=recv_other,
-        device_id=(me, 1 - half), device_id_type=MESH)
-    across.start()
 
     axial = geom_ref[0:1, :] - MIDDLE
     cosine = geom_ref[1:2, :]
@@ -88,8 +79,16 @@
         for level, piece in enumerate(split_three(part)):
             flat[3 * at + level:3 * at + level + 1, :] = piece
     pieces[0] = flat[0:PIECES, :].astype(jnp.bfloat16)
+    pl.semaphore_wait(barrier, n if reduce_here else 7)
     for slot, target in targets:
         geom_copy(pieces.at[0], slot, target).start()
+    for slot, target in targets:
+        dirs_copy(dirs_ref, slot, target).start()
+    across = pltpu.make_async_remote_copy(
+        src_ref=dirs_ref, dst_ref=other, send_sem=send_other, recv_sem=recv_other,
+        device_id=(me, 1 - half), device_id_type=MESH)
+    across.start()
+
     dirs[0] = dirs_ref[...]
 
     flat[...] = jnp.zeros_like(flat)

time: 73.3 us -> 73.3 us (level)
  no operation moved by 1% of the time
where the time goes in v6:
time: 73.3 us; the launch traced here: 73.1 us
  Pallas kernels  68.2 us (93%)
  local copies, waits for them, and re-layouts  3.35 us (5%)
  other arithmetic  0.78 us (1%)
    pallas_call x1, Pallas kernels, shards(): pl.pallas_call(functools.partial(panel_kernel, n, reduce_here), out_shape...  68.2 us
    unnamed x8, local copies, waits for them, and re-layouts  3.35 us

profile of v6, /device:TPU:0, one launch (start us, length us, event | category | flops | bytes accessed | tf_op | source)
XLA Modules:
  0.0 73.1 jit_solution(91302452185198125)
XLA Ops:
  0.6 0.0 copy-start.1
  0.6 0.7 stack.28
  1.3 0.0 copy-done.1
  1.3 0.0 copy-start.2
  1.3 0.7 copy-done.2
  2.1 0.0 copy-start
  2.1 1.0 %copy-done = bf16[2048,128]{1,0:T(8,128)(2,1)S(1)} copy-done((bf16[2048,128]{1,0:T(8,128)(2,1)S(1)}, bf16[2048,128]{1,0:T(8,128)(2,1)}, u32[]{:S(2)}) %copy-start) | copy-done | bytes 524312
  3.2 68.2 %panels.1 = (f32[2048,128]{1,0:T(8,128)S(1)}, f32[256,128]{1,0:T(8,128)S(1)}) custom-call(bf16[2048,128]{1,0:T(8,128)(2,1)S(1)} %copy-done, f32[4,2048]{1,0:T(4,128)S(1)} %pad_maximum_fusion.geom_ref), custom_call_target="tpu_custom_call" | custom-call | flops 10334765056 | bytes 1048576 | tf_op jit(solution)/shard_map/panels/pallas_call | solution.py:209
  71.4 1.0 %copy.8 = f32[2048,128]{1,0:T(8,128)} copy(f32[2048,128]{1,0:T(8,128)S(1)} %get-tuple-element.6) | data formatting | bytes 2097152
  72.4 0.7 copy.9
  (3 shorter events, 0.1 us)
Async XLA Ops:
  0.6 0.7 copy-start.1
  1.3 0.7 copy-start.2
  2.1 1.0 %copy-start = (bf16[2048,128]{1,0:T(8,128)(2,1)S(1)}, bf16[2048,128]{1,0:T(8,128)(2,1)}, u32[]{:S(2)}) copy-start(bf16[2048,128]{1,0:T(8,128)(2,1)} %dirs_ref.1) | copy-start | bytes 1572868

commit v7 on v6

--- a/solution.py
+++ b/solution.py
@@ -8,8 +8,8 @@
 from jax.sharding import PartitionSpec as P
 
 MESH = pl.DeviceIdType.MESH
-COL_STEP = 256
-COL_GROUP = 1024
+COL_STEP = 512
+ROW_STEP = 512
 MIDDLE = 4.0
 SOFTEN = 0.01
 PIECES = 16
@@ -25,7 +25,7 @@
 
 def panel_kernel(
     n, reduce_here, dirs_ref, geom_ref, product_ref, gram_ref,
-    dirs, other, pieces, rows, flat, partial, landed, summed,
+    dirs, other, pieces, rows, turned_product, flat, partial, landed, summed,
     send_dirs, recv_dirs, send_geom, recv_geom, send_other, recv_other,
     send_part, recv_part, send_sum, recv_sum,
 ):
@@ -82,14 +82,15 @@
     pl.semaphore_wait(barrier, n if reduce_here else 7)
     for slot, target in targets:
         geom_copy(pieces.at[0], slot, target).start()
+    for start in range(0, count, 128):
+        strip = dirs_ref[start:start + 128, :].astype(jnp.float32)
+        dirs[0, :, start:start + 128] = strip.T.astype(jnp.bfloat16)
     for slot, target in targets:
-        dirs_copy(dirs_ref, slot, target).start()
+        dirs_copy(dirs.at[0], slot, target).start()
     across = pltpu.make_async_remote_copy(
-        src_ref=dirs_ref, dst_ref=other, send_sem=send_other, recv_sem=recv_other,
+        src_ref=dirs.at[0], dst_ref=other, send_sem=send_other, recv_sem=recv_other,
         device_id=(me, 1 - half), device_id_type=MESH)
     across.start()
-
-    dirs[0] = dirs_ref[...]
 
     flat[...] = jnp.zeros_like(flat)
     for at, part in enumerate(row_parts):
@@ -97,41 +98,34 @@
             for spot in range(3):
                 place = PIECES * level + 3 * at + spot
                 flat[place:place + 1, :] = piece
-    for start in range(0, count, 128):
-        turned = flat[:, start:start + 128].T
-        rows[start:start + 128, :] = turned[:, :3 * PIECES].astype(jnp.bfloat16)
-    product_ref[...] = jnp.zeros_like(product_ref)
+    rows[...] = flat[0:3 * PIECES, :].astype(jnp.bfloat16)
+    turned_product[...] = jnp.zeros_like(turned_product)
 
     def tile(slot):
         def step(at, carry):
-            base = at * COL_GROUP
-            row_feature = rows[...]
-
-            def here(start):
-                return pl.ds(pl.multiple_of(base + start, COL_STEP), COL_STEP)
+            here = pl.ds(pl.multiple_of(at * COL_STEP, COL_STEP), COL_STEP)
+            part = pieces[slot, :, here].astype(jnp.float32)
+            col_feature = jnp.concatenate([part, part, part], axis=0).T.astype(jnp.bfloat16)
+            block_dirs = dirs[slot, :, here]
 
             def squares(start):
-                part = pieces[slot, :, here(start)]
-                col_feature = jnp.concatenate([part, part, part], axis=0)
-                return jnp.dot(row_feature, col_feature, preferred_element_type=jnp.float32)
-
-            total = product_ref[...]
+                return jnp.dot(col_feature, rows[:, start:start + ROW_STEP], preferred_element_type=jnp.float32)
+
             square = squares(0)
-            for start in range(0, COL_GROUP, COL_STEP):
-                ahead = squares(start + COL_STEP) if start + COL_STEP < COL_GROUP else None
+            for start in range(0, count, ROW_STEP):
+                ahead = squares(start + ROW_STEP) if start + ROW_STEP < count else None
                 values = lax.rsqrt(square).astype(jnp.bfloat16)
-                total = total + jnp.dot(
-                    values, dirs[slot, here(start), :], preferred_element_type=jnp.float32)
+                turned_product[:, start:start + ROW_STEP] += jnp.dot(
+                    block_dirs, values, preferred_element_type=jnp.float32)
                 square = ahead
-            product_ref[...] = total
             return carry
 
-        lax.fori_loop(0, count // COL_GROUP, step, 0)
+        lax.fori_loop(0, count // COL_STEP, step, 0)
 
     def turn(slot, carry):
         @pl.when(slot > 0)
         def _():
-            dirs_copy(dirs_ref, slot, pair).wait_recv()
+            dirs_copy(dirs.at[0], slot, pair).wait_recv()
             geom_copy(pieces.at[0], slot, pair).wait_recv()
 
         @pl.when((slot == 2) | (slot == 3))
@@ -145,14 +139,15 @@
     lax.fori_loop(0, SLOTS, turn, 0)
 
     across.wait()
+    for start in range(0, count, 128):
+        product_ref[start:start + 128, :] = turned_product[:, start:start + 128].T
     total = product_ref[...]
     high = total.astype(jnp.bfloat16)
     low = (total - high.astype(jnp.float32)).astype(jnp.bfloat16)
     inverse = 1.0 / (count * n)
     for place, value in ((half, dirs[0]), (1 - half, other[...])):
-        turned = value.T
-        inner = jnp.dot(turned, high, preferred_element_type=jnp.float32)
-        inner = inner + jnp.dot(turned, low, preferred_element_type=jnp.float32)
+        inner = jnp.dot(value, high, preferred_element_type=jnp.float32)
+        inner = inner + jnp.dot(value, low, preferred_element_type=jnp.float32)
         partial[pl.ds(pl.multiple_of(place * width, width), width), :] = inner * inverse
 
     if reduce_here:
@@ -195,7 +190,7 @@
         gram_ref[...] = partial[...]
 
     for slot in range(1, SLOTS):
-        dirs_copy(dirs_ref, slot, pair).wait_send()
+        dirs_copy(dirs.at[0], slot, pair).wait_send()
         geom_copy(pieces.at[0], slot, pair).wait_send()
 
 
@@ -215,10 +210,11 @@
         in_specs=[vmem, vmem],
         out_specs=(vmem, vmem),
         scratch_shapes=[
-            pltpu.VMEM((SLOTS, count, width), jnp.bfloat16),
-            pltpu.VMEM((count, width), jnp.bfloat16),
+            pltpu.VMEM((SLOTS, width, count), jnp.bfloat16),
+            pltpu.VMEM((width, count), jnp.bfloat16),
             pltpu.VMEM((SLOTS, PIECES, count), jnp.bfloat16),
-            pltpu.VMEM((count, 3 * PIECES), jnp.bfloat16),
+            pltpu.VMEM((3 * PIECES, count), jnp.bfloat16),
+            pltpu.VMEM((width, count), jnp.float32),
             pltpu.VMEM((128, count), jnp.float32),
             pltpu.VMEM((2 * width, width), jnp.float32),
             pltpu.VMEM((n, depth, width), jnp.float32),

time: 73.3 us -> 70.4 us (0.960)
  Pallas kernels: 68.2 us -> 65.3 us
    pallas_call x1, Pallas kernels: 68.2 us -> 65.3 us  [shards(): pl.pallas_call(functools.partial(panel_kernel, n, reduce_here), out_shape...]
where the time goes in v7:
time: 70.4 us; the launch traced here: 70.1 us
  Pallas kernels  65.3 us (93%)
  local copies, waits for them, and re-layouts  3.35 us (5%)
  other arithmetic  0.78 us (1%)
    pallas_call x1, Pallas kernels, shards(): pl.pallas_call(functools.partial(panel_kernel, n, reduce_here), out_shape...  65.3 us
    unnamed x8, local copies, waits for them, and re-layouts  3.35 us

profile of v7, /device:TPU:0, one launch (start us, length us, event | category | flops | bytes accessed | tf_op | source)
XLA Modules:
  0.0 70.1 jit_solution(14873042466186277041)
XLA Ops:
  0.6 0.0 copy-start.1
  0.6 0.7 stack.28
  1.3 0.0 copy-done.1
  1.3 0.0 copy-start.2
  1.3 0.7 copy-done.2
  2.1 0.0 copy-start
  2.1 1.0 %copy-done = bf16[2048,128]{1,0:T(8,128)(2,1)S(1)} copy-done((bf16[2048,128]{1,0:T(8,128)(2,1)S(1)}, bf16[2048,128]{1,0:T(8,128)(2,1)}, u32[]{:S(2)}) %copy-start) | copy-done | bytes 524312
  3.2 65.3 %panels.1 = (f32[2048,128]{1,0:T(8,128)S(1)}, f32[256,128]{1,0:T(8,128)S(1)}) custom-call(bf16[2048,128]{1,0:T(8,128)(2,1)S(1)} %copy-done, f32[4,2048]{1,0:T(4,128)S(1)} %pad_maximum_fusion.geom_ref), custom_call_target="tpu_custom_call" | custom-call | flops 10334765056 | bytes 1048576 | tf_op jit(solution)/shard_map/panels/pallas_call | solution.py:204
  68.5 1.0 %copy.8 = f32[2048,128]{1,0:T(8,128)} copy(f32[2048,128]{1,0:T(8,128)S(1)} %get-tuple-element.6) | data formatting | bytes 2097152
  69.5 0.7 copy.9
  (3 shorter events, 0.1 us)
Async XLA Ops:
  0.6 0.7 %copy-start.1 = (bf16[2048]{0:T(1024)(128)(2,1)S(1)}, bf16[2048]{0:T(1024)(128)(2,1)}, u32[]{:S(2)}) copy-start(bf16[2048]{0:T(1024)(128)(2,1)} %param.7) | copy-start | bytes 12292
  1.3 0.7 copy-start.2
  2.1 1.0 %copy-start = (bf16[2048,128]{1,0:T(8,128)(2,1)S(1)}, bf16[2048,128]{1,0:T(8,128)(2,1)}, u32[]{:S(2)}) copy-start(bf16[2048,128]{1,0:T(8,128)(2,1)} %dirs_ref.1) | copy-start | bytes 1572868

commit v8 on v7

--- a/solution.py
+++ b/solution.py
@@ -10,6 +10,7 @@
 MESH = pl.DeviceIdType.MESH
 COL_STEP = 512
 ROW_STEP = 512
+CUT = 32
 MIDDLE = 4.0
 SOFTEN = 0.01
 PIECES = 16
@@ -85,12 +86,25 @@
     for start in range(0, count, 128):
         strip = dirs_ref[start:start + 128, :].astype(jnp.float32)
         dirs[0, :, start:start + 128] = strip.T.astype(jnp.bfloat16)
-    for slot, target in targets:
-        dirs_copy(dirs.at[0], slot, target).start()
-    across = pltpu.make_async_remote_copy(
-        src_ref=dirs.at[0], dst_ref=other, send_sem=send_other, recv_sem=recv_other,
-        device_id=(me, 1 - half), device_id_type=MESH)
-    across.start()
+    def cut_copy(source, slot, target, first):
+        return pltpu.make_async_remote_copy(
+            src_ref=dirs.at[source, first:first + CUT], dst_ref=dirs.at[slot, first:first + CUT],
+            send_sem=send_dirs.at[slot], recv_sem=recv_dirs.at[slot],
+            device_id=(target, half), device_id_type=MESH)
+
+    def across_copy(first, depth):
+        return pltpu.make_async_remote_copy(
+            src_ref=dirs.at[0, first:first + depth], dst_ref=other.at[first:first + depth],
+            send_sem=send_other, recv_sem=recv_other,
+            device_id=(me, 1 - half), device_id_type=MESH)
+
+    for group in (targets[:1], targets[1:3], targets[3:]):
+        for first in range(0, width, CUT):
+            for slot, target in group:
+                cut_copy(0, slot, target, first).start()
+            if group[0][0] == 6:
+                across_copy(first, CUT).start()
+    across = across_copy(0, width)
 
     flat[...] = jnp.zeros_like(flat)
     for at, part in enumerate(row_parts):
@@ -130,7 +144,8 @@
 
         @pl.when((slot == 2) | (slot == 3))
         def _():
-            dirs_copy(dirs.at[slot], slot + 2, pair).start()
+            for first in range(0, width, CUT):
+                cut_copy(slot, slot + 2, pair, first).start()
             geom_copy(pieces.at[slot], slot + 2, pair).start()
 
         tile(slot)

time: 70.4 us -> 70.4 us (level)
  no operation moved by 1% of the time
where the time goes in v8:
time: 70.4 us; the launch traced here: 70.2 us
  Pallas kernels  65.4 us (93%)
  local copies, waits for them, and re-layouts  3.35 us (5%)
  other arithmetic  0.78 us (1%)
    pallas_call x1, Pallas kernels, shards(): pl.pallas_call(functools.partial(panel_kernel, n, reduce_here), out_shape...  65.4 us
    unnamed x8, local copies, waits for them, and re-layouts  3.35 us

profile of v8, /device:TPU:0, one launch (start us, length us, event | category | flops | bytes accessed | tf_op | source)
XLA Modules:
  0.0 70.2 jit_solution(17342907657512337539)
XLA Ops:
  0.6 0.0 copy-start.1
  0.6 0.7 stack.28
  1.3 0.0 copy-done.1
  1.3 0.0 copy-start.2
  1.3 0.7 copy-done.2
  2.1 0.0 copy-start
  2.1 1.0 %copy-done = bf16[2048,128]{1,0:T(8,128)(2,1)S(1)} copy-done((bf16[2048,128]{1,0:T(8,128)(2,1)S(1)}, bf16[2048,128]{1,0:T(8,128)(2,1)}, u32[]{:S(2)}) %copy-start) | copy-done | bytes 524312
  3.2 65.4 %panels.1 = (f32[2048,128]{1,0:T(8,128)S(1)}, f32[256,128]{1,0:T(8,128)S(1)}) custom-call(bf16[2048,128]{1,0:T(8,128)(2,1)S(1)} %copy-done, f32[4,2048]{1,0:T(4,128)S(1)} %pad_maximum_fusion.geom_ref), custom_call_target="tpu_custom_call" | custom-call | flops 10334765056 | bytes 1048576 | tf_op jit(solution)/shard_map/panels/pallas_call | solution.py:219
  68.6 1.0 %copy.8 = f32[2048,128]{1,0:T(8,128)} copy(f32[2048,128]{1,0:T(8,128)S(1)} %get-tuple-element.6) | data formatting | bytes 2097152
  69.5 0.7 copy.9
  (3 shorter events, 0.1 us)
Async XLA Ops:
  0.6 0.7 %copy-start.1 = (bf16[2048]{0:T(1024)(128)(2,1)S(1)}, bf16[2048]{0:T(1024)(128)(2,1)}, u32[]{:S(2)}) copy-start(bf16[2048]{0:T(1024)(128)(2,1)} %param.7) | copy-start | bytes 12292
  1.3 0.7 copy-start.2
  2.1 1.0 %copy-start = (bf16[2048,128]{1,0:T(8,128)(2,1)S(1)}, bf16[2048,128]{1,0:T(8,128)(2,1)}, u32[]{:S(2)}) copy-start(bf16[2048,128]{1,0:T(8,128)(2,1)} %dirs_ref.1) | copy-start | bytes 1572868

commit v9 on v7

--- a/solution.py
+++ b/solution.py
@@ -114,7 +114,7 @@
             square = squares(0)
             for start in range(0, count, ROW_STEP):
                 ahead = squares(start + ROW_STEP) if start + ROW_STEP < count else None
-                values = lax.rsqrt(square).astype(jnp.bfloat16)
+                values = lax.rsqrt(square.astype(jnp.bfloat16))
                 turned_product[:, start:start + ROW_STEP] += jnp.dot(
                     block_dirs, values, preferred_element_type=jnp.float32)
                 square = ahead

time: 70.4 us -> 75.5 us (1.072)
  Pallas kernels: 65.3 us -> 70.5 us
    pallas_call x1, Pallas kernels: 65.3 us -> 70.5 us  [shards(): pl.pallas_call(functools.partial(panel_kernel, n, reduce_here), out_shape...]
where the time goes in v9:
time: 75.5 us; the launch traced here: 75.3 us
  Pallas kernels  70.5 us (93%)
  local copies, waits for them, and re-layouts  3.35 us (4%)
  other arithmetic  0.78 us (1%)
    pallas_call x1, Pallas kernels, shards(): pl.pallas_call(functools.partial(panel_kernel, n, reduce_here), out_shape...  70.5 us
    unnamed x8, local copies, waits for them, and re-layouts  3.35 us

profile of v9, /device:TPU:0, one launch (start us, length us, event | category | flops | bytes accessed | tf_op | source)
XLA Modules:
  0.0 75.3 jit_solution(1784935675762477743)
XLA Ops:
  0.6 0.0 copy-start.1
  0.6 0.7 stack.28
  1.3 0.0 copy-done.1
  1.3 0.0 copy-start.2
  1.3 0.7 copy-done.2
  2.1 0.0 copy-start
  2.1 1.0 %copy-done = bf16[2048,128]{1,0:T(8,128)(2,1)S(1)} copy-done((bf16[2048,128]{1,0:T(8,128)(2,1)S(1)}, bf16[2048,128]{1,0:T(8,128)(2,1)}, u32[]{:S(2)}) %copy-start) | copy-done | bytes 524312
  3.2 70.5 %panels.1 = (f32[2048,128]{1,0:T(8,128)S(1)}, f32[256,128]{1,0:T(8,128)S(1)}) custom-call(bf16[2048,128]{1,0:T(8,128)(2,1)S(1)} %copy-done, f32[4,2048]{1,0:T(4,128)S(1)} %pad_maximum_fusion.geom_ref), custom_call_target="tpu_custom_call" | custom-call | flops 10334765056 | bytes 1048576 | tf_op jit(solution)/shard_map/panels/pallas_call | solution.py:204
  73.7 1.0 %copy.8 = f32[2048,128]{1,0:T(8,128)} copy(f32[2048,128]{1,0:T(8,128)S(1)} %get-tuple-element.6) | data formatting | bytes 2097152
  74.6 0.7 copy.9
  (3 shorter events, 0.1 us)
Async XLA Ops:
  0.6 0.7 copy-start.1
  1.3 0.7 copy-start.2
  2.1 1.0 %copy-start = (bf16[2048,128]{1,0:T(8,128)(2,1)S(1)}, bf16[2048,128]{1,0:T(8,128)(2,1)}, u32[]{:S(2)}) copy-start(bf16[2048,128]{1,0:T(8,128)(2,1)} %dirs_ref.1) | copy-start | bytes 1572868

commit v10 on v7

--- a/solution.py
+++ b/solution.py
@@ -9,7 +9,8 @@
 
 MESH = pl.DeviceIdType.MESH
 COL_STEP = 512
-ROW_STEP = 512
+ROW_STEP = 256
+COL_GROUP = 1024
 MIDDLE = 4.0
 SOFTEN = 0.01
 PIECES = 16
@@ -103,24 +104,28 @@
 
     def tile(slot):
         def step(at, carry):
-            here = pl.ds(pl.multiple_of(at * COL_STEP, COL_STEP), COL_STEP)
-            part = pieces[slot, :, here].astype(jnp.float32)
-            col_feature = jnp.concatenate([part, part, part], axis=0).T.astype(jnp.bfloat16)
-            block_dirs = dirs[slot, :, here]
-
-            def squares(start):
-                return jnp.dot(col_feature, rows[:, start:start + ROW_STEP], preferred_element_type=jnp.float32)
-
-            square = squares(0)
-            for start in range(0, count, ROW_STEP):
-                ahead = squares(start + ROW_STEP) if start + ROW_STEP < count else None
+            features, block_dirs, chunks = [], [], []
+            for sub in range(COL_GROUP // COL_STEP):
+                here = pl.ds(pl.multiple_of(at * COL_GROUP + sub * COL_STEP, COL_STEP), COL_STEP)
+                part = pieces[slot, :, here].astype(jnp.float32)
+                features.append(jnp.concatenate([part, part, part], axis=0).T.astype(jnp.bfloat16))
+                block_dirs.append(dirs[slot, :, here])
+                chunks += [(sub, start) for start in range(0, count, ROW_STEP)]
+
+            def squares(chunk):
+                sub, start = chunk
+                return jnp.dot(features[sub], rows[:, start:start + ROW_STEP], preferred_element_type=jnp.float32)
+
+            square = squares(chunks[0])
+            for (sub, start), following in zip(chunks, chunks[1:] + [None]):
+                ahead = squares(following) if following else None
                 values = lax.rsqrt(square).astype(jnp.bfloat16)
                 turned_product[:, start:start + ROW_STEP] += jnp.dot(
-                    block_dirs, values, preferred_element_type=jnp.float32)
+                    block_dirs[sub], values, preferred_element_type=jnp.float32)
                 square = ahead
             return carry
 
-        lax.fori_loop(0, count // COL_STEP, step, 0)
+        lax.fori_loop(0, count // COL_GROUP, step, 0)
 
     def turn(slot, carry):
         @pl.when(slot > 0)

time: 70.4 us -> 72.9 us (1.036)
  Pallas kernels: 65.3 us -> 67.9 us
    pallas_call x1, Pallas kernels: 65.3 us -> 67.9 us  [shards(): pl.pallas_call(functools.partial(panel_kernel, n, reduce_here), out_shape...]
where the time goes in v10:
time: 72.9 us; the launch traced here: 72.7 us
  Pallas kernels  67.9 us (93%)
  local copies, waits for them, and re-layouts  3.35 us (5%)
  other arithmetic  0.78 us (1%)
    pallas_call x1, Pallas kernels, shards(): pl.pallas_call(functools.partial(panel_kernel, n, reduce_here), out_shape...  67.9 us
    unnamed x8, local copies, waits for them, and re-layouts  3.35 us

profile of v10, /device:TPU:0, one launch (start us, length us, event | category | flops | bytes accessed | tf_op | source)
XLA Modules:
  0.0 72.7 jit_solution(17796310204415670479)
XLA Ops:
  0.6 0.0 copy-start.1
  0.6 0.7 stack.28
  1.3 0.0 copy-done.1
  1.3 0.0 copy-start.2
  1.3 0.7 copy-done.2
  2.1 0.0 copy-start
  2.1 1.0 %copy-done = bf16[2048,128]{1,0:T(8,128)(2,1)S(1)} copy-done((bf16[2048,128]{1,0:T(8,128)(2,1)S(1)}, bf16[2048,128]{1,0:T(8,128)(2,1)}, u32[]{:S(2)}) %copy-start) | copy-done | bytes 524312
  3.2 67.9 %panels.1 = (f32[2048,128]{1,0:T(8,128)S(1)}, f32[256,128]{1,0:T(8,128)S(1)}) custom-call(bf16[2048,128]{1,0:T(8,128)(2,1)S(1)} %copy-done, f32[4,2048]{1,0:T(4,128)S(1)} %pad_maximum_fusion.geom_ref), custom_call_target="tpu_custom_call" | custom-call | flops 10334765056 | bytes 1048576 | tf_op jit(solution)/shard_map/panels/pallas_call | solution.py:209
  71.0 1.0 %copy.8 = f32[2048,128]{1,0:T(8,128)} copy(f32[2048,128]{1,0:T(8,128)S(1)} %get-tuple-element.6) | data formatting | bytes 2097152
  72.0 0.7 copy.9
  (3 shorter events, 0.1 us)
Async XLA Ops:
  0.6 0.7 copy-start.1
  1.3 0.7 copy-start.2
  2.1 1.0 %copy-start = (bf16[2048,128]{1,0:T(8,128)(2,1)S(1)}, bf16[2048,128]{1,0:T(8,128)(2,1)}, u32[]{:S(2)}) copy-start(bf16[2048,128]{1,0:T(8,128)(2,1)} %dirs_ref.1) | copy-start | bytes 1572868
